TPU v7x, 512 devices: a whole 4x4x16 slice. The times are simulated.
512 devices in a mesh: seq: 32 (over z, x_lo), tp: 16 (over x_hi, y, core).
Axes of the slice: x: 4 (x_hi: 2, x_lo: 2; x = x_hi * 2 + x_lo), y: 4, z: 16, core: 2. Of those that a mesh axis runs over, the one named last changes fastest.
Arguments:
- tokens: bfloat16 [256, 8192], P('tp', 'seq'), may hold values from -6 to 6
- grad_out: bfloat16 [256, 8192], P('tp', 'seq'), may hold values from -6 to 6
- gate_values: bfloat16 [8192, 28672], P('seq', 'tp'), may hold values from -0.0625 to 0.0625
- up_values: bfloat16 [8192, 28672], P('seq', 'tp'), may hold values from -0.0625 to 0.0625
- down_values: bfloat16 [28672, 8192], P('tp', 'seq'), may hold values from -0.03125 to 0.03125
- gate_scales: float32 [64, 224], P('seq', 'tp'), may hold values from 0.5 to 2
- up_scales: float32 [64, 224], P('seq', 'tp'), may hold values from 0.5 to 2
- down_scales: float32 [224, 64], P('tp', 'seq'), may hold values from 0.5 to 2
Outputs:
- mixed: bfloat16 [256, 8192], P('tp', 'seq')
- input_grad: bfloat16 [256, 8192], P('tp', 'seq')
All inputs are finite; a program needn't handle non-finite values.
Results may differ from a plain program's by a relative error of at most 0.0072.
Values may be sent and summed in bfloat16 or wider, within the bound.
No kernel may reach another device: no remote copies, remote signals or barrier semaphores. Data moves between devices by JAX's collectives and lax.ppermute only.
A program may use at most 64 MiB of HBM per device.

v0:
```python
import jax
import jax.numpy as jnp
from jax import lax
from jax.sharding import PartitionSpec as P

BLK = 128


def dequantize(values, scales):
    spread = jnp.repeat(jnp.repeat(scales, BLK, axis=0), BLK, axis=1)
    return (values.astype(jnp.float32) * spread).astype(jnp.bfloat16)


def gated_unit(gate_sum, up_sum, back_sum):
    sig = jax.nn.sigmoid(gate_sum)
    active = gate_sum * sig
    hidden = (active * up_sum).astype(jnp.bfloat16)
    gate_grad = (back_sum * up_sum * (sig * (1.0 + gate_sum * (1.0 - sig)))).astype(jnp.bfloat16)
    up_grad = (back_sum * active).astype(jnp.bfloat16)
    return (hidden, jnp.concatenate((gate_grad, up_grad), axis=1))


def transposed(left, right):
    return lax.dot_general(
        left, right, (((1,), (1,)), ((), ())), preferred_element_type=jnp.float32
    )


def shards(
    tokens, grad_out, gate_values, up_values, down_values, gate_scales, up_scales, down_scales
):
    w_gate = dequantize(gate_values, gate_scales)
    w_up = dequantize(up_values, up_scales)
    w_down = dequantize(down_values, down_scales)
    w_pair = jnp.concatenate((w_gate, w_up), axis=1)
    hidden_cols = w_gate.shape[1]
    all_rows, all_grads = (
        lax.all_gather(tokens, "tp", axis=0, tiled=True),
        lax.all_gather(grad_out, "tp", axis=0, tiled=True),
    )
    block = all_rows
    pair_sum = lax.psum_scatter(
        jnp.dot(block, w_pair, preferred_element_type=jnp.float32),
        "seq",
        scatter_dimension=0,
        tiled=True,
    )
    block = all_grads
    back_sum = lax.psum_scatter(transposed(block, w_down), "seq", scatter_dimension=0, tiled=True)
    hidden, joint_grad = gated_unit(pair_sum[:, :hidden_cols], pair_sum[:, hidden_cols:], back_sum)
    mixed_term = jnp.dot(
        lax.all_gather(hidden, "seq", axis=0, tiled=True),
        w_down,
        preferred_element_type=jnp.float32,
    )
    input_term = transposed(lax.all_gather(joint_grad, "seq", axis=0, tiled=True), w_pair)
    mixed, input_grad = (
        lax.psum_scatter(mixed_term, "tp", scatter_dimension=0, tiled=True),
        lax.psum_scatter(input_term, "tp", scatter_dimension=0, tiled=True),
    )
    return (mixed.astype(jnp.bfloat16), input_grad.astype(jnp.bfloat16))


def solution(mesh):
    return jax.shard_map(
        shards,
        mesh=mesh,
        in_specs=(
            P("tp", "seq"),
            P("tp", "seq"),
            P("seq", "tp"),
            P("seq", "tp"),
            P("tp", "seq"),
            P("seq", "tp"),
            P("seq", "tp"),
            P("tp", "seq"),
        ),
        out_specs=(P("tp", "seq"), P("tp", "seq")),
        check_vma=False,
    )
```

profile of v0, /device:TPU:1, one launch (start us, length us, event | category | flops | bytes accessed | tf_op | source)
XLA Modules:
  0.0 645.6 jit_solution(8554824412164097153)
XLA Ops:
  7.2 0.8 copy.33
  8.0 26.3 %all_gather.14 = bf16[256,256]{1,0:T(8,128)(2,1)S(1)} all-gather(bf16[16,256]{1,0:T(8,128)(2,1)} %param.9), channel_id=1, replica_groups=mesh['seq'=32,'tp'=16] {'tp'}, dimensions={0}, use_global_device_ids=true | all-gather | bytes 139264 | tf_op jit(solution)/shard_map/all_gather | solution.py:39
  34.4 2.2 broadcast_in_dim.23
  36.5 1.7 convolution_bitcast_fusion.1
  38.3 2.8 copy.38
  41.1 1.1 copy-done.2
  42.2 1.3 copy.27
  43.5 2.2 copy.29
  46.2 1.8 fusion.1
  48.0 21.2 %all_gather.12 = bf16[256,256]{1,0:T(8,128)(2,1)S(1)} all-gather(bf16[16,256]{1,0:T(8,128)(2,1)S(1)} %copy-done.3), channel_id=1, replica_groups=mesh['seq'=32,'tp'=16] {'tp'}, dimensions={0}, use_global_device_ids=true | all-gather | bytes 139264 | tf_op jit(solution)/shard_map/all_gather | solution.py:38
  69.2 2.5 convolution_bitcast_fusion
  71.7 5.2 copy.36
  76.9 78.8 %reduce-scatter.15.cloned.1.call-done = f32[8,1792]{1,0:T(8,128)} async-done(((f32[256,1792]{1,0:T(8,128)}), f32[8,1792]{1,0:T(8,128)}) %reduce-scatter.15.cloned.1.call-update) | async-done | bytes 57360 | tf_op jit(solution)/shard_map/reduce_scatter | solution.py:49
  155.7 144.6 %reduce-scatter.13.cloned.1.call-done = f32[8,3584]{1,0:T(8,128)} async-done(((f32[256,3584]{1,0:T(8,128)}), f32[8,3584]{1,0:T(8,128)}) %reduce-scatter.13.cloned.1.call-update) | async-done | bytes 114704 | tf_op jit(solution)/shard_map/reduce_scatter | solution.py:42
  300.3 0.9 multiply_convert_fusion.1
  301.2 0.6 pad_maximum_fusion.3
  301.9 53.8 %all_gather.13 = bf16[256,1792]{1,0:T(8,128)(2,1)S(1)} all-gather(bf16[8,1792]{1,0:T(8,128)(2,1)S(1)} %get-tuple-element.4), channel_id=1, replica_groups=mesh['seq'=32,'tp'=16] {'seq'}, dimensions={0}, use_global_device_ids=true | all-gather | bytes 946176 | tf_op jit(solution)/shard_map/all_gather | solution.py:52
  355.8 2.3 fusion.8
  358.2 77.8 %all-gather.2.cloned.1.call-done = bf16[256,3584]{1,0:T(8,128)(2,1)} async-done(((bf16[8,3584]{1,0:T(8,128)(2,1)}), bf16[256,3584]{1,0:T(8,128)(2,1)}) %all-gather.2.cloned.1.call-update) | async-done | bytes 1835024 | tf_op jit(solution)/shard_map/all_gather | solution.py:56
  435.9 3.1 fusion.3
  439.0 107.0 %reduce-scatter.9.cloned.1.call-done = f32[16,256]{1,0:T(8,128)} async-done(((f32[256,256]{1,0:T(8,128)}), f32[16,256]{1,0:T(8,128)}) %reduce-scatter.9.cloned.1.call-update) | async-done | bytes 16400 | tf_op jit(solution)/shard_map/reduce_scatter | solution.py:58
  546.0 1.3 convert_element_type.40
  547.3 90.4 %reduce-scatter.11.cloned.1.call-done = f32[16,256]{1,0:T(8,128)} async-done(((f32[256,256]{1,0:T(8,128)}), f32[16,256]{1,0:T(8,128)}) %reduce-scatter.11.cloned.1.call-update) | async-done | bytes 16400 | tf_op jit(solution)/shard_map/reduce_scatter | solution.py:59
  637.8 1.3 convert_element_type.43
  (30 shorter events, 0.7 us)
Async XLA Ops:
  7.2 148.6 %reduce-scatter.15.cloned.1.call-start = ((), (), s32[]{:S(2)}) async-start(), calls=%async_computation.8 | async-start | bytes 1892352 | tf_op jit(solution)/shard_map/reduce_scatter | solution.py:49
  34.3 2.3 copy-start.1
  41.0 1.2 copy-start.2
  41.1 4.7 copy-start.4
  41.1 4.8 copy-start.5
  41.1 259.2 %reduce-scatter.13.cloned.1.call-start = ((), (), s32[]{:S(2)}) async-start(), calls=%async_computation.7 | async-start | bytes 3784704 | tf_op jit(solution)/shard_map/reduce_scatter | solution.py:42
  46.1 1.8 copy-start.3
  48.0 21.2 %copy-start = (bf16[256,1792]{0,1:T(8,128)(2,1)}, bf16[256,1792]{0,1:T(8,128)(2,1)S(1)}, u32[]{:S(2)}) copy-start(bf16[256,1792]{0,1:T(8,128)(2,1)S(1)} %get-tuple-element.6) | copy-start | bytes 2752516
  76.8 359.1 %all-gather.2.cloned.1.call-start = ((), (), s32[]{:S(2)}) async-start(), calls=%async_computation.5 | async-start | bytes 1892352 | tf_op jit(solution)/shard_map/all_gather | solution.py:56
  301.9 244.1 %reduce-scatter.9.cloned.1.call-start = ((), (), s32[]{:S(2)}) async-start(), calls=%async_computation.4 | async-start | bytes 278528 | tf_op jit(solution)/shard_map/reduce_scatter | solution.py:58
  358.1 279.7 %reduce-scatter.11.cloned.1.call-start = ((), (), s32[]{:S(2)}) async-start(), calls=%async_computation.6 | async-start | bytes 278528 | tf_op jit(solution)/shard_map/reduce_scatter | solution.py:59
Sparse Core Ops, SparseCore 0:
  41.2 114.4 reduce-scatter.14
  158.8 141.4 reduce-scatter.12
  302.4 133.4 all-gather.1
  440.3 105.6 reduce-scatter.8
  550.4 87.3 reduce-scatter.10
where the time goes:
time: 647 us; the launch traced here: 646 us
  waiting for transfers between devices  499 us (77%)
  blocking collectives  101 us (16%)
  local copies, waits for them, and re-layouts  15.9 us (2%)
  between operations  13.9 us (2%)
  matrix products  9.6 us (1%)
    reduce_scatter x1, waiting for transfers between devices, shards(): lax.psum_scatter(jnp.dot(block, w_pair, preferred_element_type=jnp.float3...  145 us
    reduce_scatter x1, waiting for transfers between devices, shards(): lax.psum_scatter(mixed_term, 'tp', scatter_dimension=0, tiled=True)  107 us
    reduce_scatter x1, waiting for transfers between devices, shards(): lax.psum_scatter(input_term, 'tp', scatter_dimension=0, tiled=True)  90.4 us
    reduce_scatter x1, waiting for transfers between devices, shards(): lax.psum_scatter(transposed(block, w_down), 'seq', scatter_dimension=0, t...  78.8 us
    all_gather x1, waiting for transfers between devices, shards(): lax.all_gather(joint_grad, 'seq', axis=0, tiled=True)  77.8 us
    all_gather x1, blocking collectives, shards(): lax.all_gather(hidden, 'seq', axis=0, tiled=True)  53.8 us
    all_gather x1, blocking collectives, shards(): lax.all_gather(grad_out, 'tp', axis=0, tiled=True)  26.3 us
    all_gather x1, blocking collectives, shards(): lax.all_gather(tokens, 'tp', axis=0, tiled=True)  21.2 us
  transfers between devices with their start and end apart: 5, of which 5 were waited for; matrix products, arithmetic and copies ran while one was open for 3% of the time, Pallas kernels for 0%

commit v1 on v0

v1 whole, which is shorter than its diff:
```python
import functools

import jax
import jax.numpy as jnp
from jax import lax
from jax.experimental import pallas as pl
from jax.experimental.pallas import tpu as pltpu
from jax.sharding import Mesh, PartitionSpec as P

BLK = 128
Z = ("zh", "zl")
TP = ("xh", "y", "core")
SEQ = ("zh", "zl", "xl")
F32, BF16 = jnp.float32, jnp.bfloat16
PARAMS = pltpu.CompilerParams(vmem_limit_bytes=24 * 1024 * 1024)
VMEM = pl.BlockSpec(memory_space=pltpu.VMEM)
SMEM = pl.BlockSpec(memory_space=pltpu.SMEM)


def call(body, out_shapes, ins, name, smem=0, scratch=()):
    return pl.pallas_call(
        body,
        out_shape=[jax.ShapeDtypeStruct(s, d) for s, d in out_shapes],
        in_specs=[SMEM] * smem + [VMEM] * (len(ins) - smem),
        out_specs=[VMEM] * len(out_shapes),
        scratch_shapes=list(scratch),
        compiler_params=PARAMS,
        name=name,
    )(*ins)


def scaled(ref, rows, cols, scale):
    return (ref[rows, cols].astype(F32) * scale).astype(BF16)


def dequant_kernel(pos, gs, us, ds, gate, up, down, gu_keep, gu_send, d_keep, d_send):
    depth, cols = gu_keep.shape[0] // 2, gu_keep.shape[1]
    blocks = cols // BLK
    for which, gu_out, d_out in ((pos[0], gu_keep, d_keep), (1 - pos[0], gu_send, d_send)):
        for j in range(blocks):
            src = which * blocks + j
            at = pl.ds(pl.multiple_of(src * BLK, BLK), BLK)
            for i in range(depth // BLK):
                rows = slice(i * BLK, (i + 1) * BLK)
                low = slice(depth + i * BLK, depth + (i + 1) * BLK)
                to = slice(j * BLK, (j + 1) * BLK)
                gu_out[rows, to] = scaled(gate, rows, at, gs[i, src])
                gu_out[low, to] = scaled(up, rows, at, us[i, src])
                d_out[to, rows] = scaled(down, at, rows, ds[src, i])


def nt(a, b):
    return lax.dot_general(a, b, (((1,), (1,)), ((), ())), preferred_element_type=F32)


def nn(a, b):
    return jnp.dot(a, b, preferred_element_type=F32)


def partial_kernel(pos, acts, gu_keep, gu_other, d_keep, d_other, plus1, minus1, plus2, minus2, own):
    xl, zl = pos[0], pos[1]
    depth = d_keep.shape[1]
    for shift, out in ((1, plus1), (3, minus1), (2, None), (0, own)):
        cls = lax.rem(zl + shift, 4)

        def rows(x, which):
            return jnp.concatenate([acts[x, ch * 4 + cls, which] for ch in range(4)], axis=0)

        tm, to = rows(xl, 0), rows(1 - xl, 0)
        gm, go = rows(xl, 1), rows(1 - xl, 1)
        parts = (
            nn(tm, gu_keep[:depth]) + nn(to, gu_other[:depth]),
            nn(tm, gu_keep[depth:]) + nn(to, gu_other[depth:]),
            nt(gm, d_keep[...]) + nt(go, d_other[...]),
        )
        for k, part in enumerate(parts):
            width = part.shape[1]
            cols = slice(k * width, (k + 1) * width)
            if out is None:
                half = part.shape[0] // 2
                plus2[:, cols] = part[:half].astype(BF16)
                minus2[:, cols] = part[half:].astype(BF16)
            else:
                out[:, cols] = part.astype(out.dtype)


def window_kernel(own, a1, b1, a2, b2, out):
    half = a2.shape[0]
    for rows, far in ((slice(0, half), a2), (slice(half, 2 * half), b2)):
        total = own[rows, :] + a1[rows, :].astype(F32) + b1[rows, :].astype(F32) + far[...].astype(F32)
        for ch in range(2):
            block = rows.start // 16 + ch
            out[block] = total[ch * 16 : (ch + 1) * 16].astype(BF16)


def gated_kernel(parts, out):
    width = parts.shape[2] // 3

    def total(k):
        cols = slice(k * width, (k + 1) * width)
        s = parts[0, :, cols].astype(F32)
        for i in range(1, parts.shape[0]):
            s = s + parts[i, :, cols].astype(F32)
        return s

    gate_sum, up_sum, back_sum = total(0), total(1), total(2)
    sig = jax.nn.sigmoid(gate_sum)
    active = gate_sum * sig
    results = (
        active * up_sum,
        back_sum * up_sum * (sig * (1.0 + gate_sum * (1.0 - sig))),
        back_sum * active,
    )
    for k, result in enumerate(results):
        for i in range(out.shape[0]):
            out[i, :, k * width : (k + 1) * width] = result.astype(BF16)


def output_kernel(pos, own, a1, b1, a2, b2, gu_keep, gu_other, d_keep, d_other, out, rows):
    xl, zl = pos[0], pos[1]
    n, half = own.shape[0], a2.shape[0]
    width = d_keep.shape[0]
    depth = d_keep.shape[1]
    rows[0:n] = own[...]
    rows[n : 2 * n] = a1[...]
    rows[2 * n : 2 * n + half] = a2[...]
    rows[2 * n + half : 3 * n] = b2[...]
    rows[3 * n : 4 * n] = b1[...]
    hidden, gate_grad, up_grad = (rows[:, k * width : (k + 1) * width] for k in range(3))
    for x, gu, d in ((xl, gu_keep, d_keep), (1 - xl, gu_other, d_other)):
        mixed = nn(hidden, d[...]).astype(BF16)
        grad = (nt(gate_grad, gu[:depth]) + nt(up_grad, gu[depth:])).astype(BF16)
        for order, shift in enumerate((0, 3, 2, 1)):
            cls = lax.rem(zl + shift, 4)
            for ch in range(4):
                at = slice(order * n + ch * 16, order * n + (ch + 1) * 16)
                out[x, ch * 4 + cls, :, 0:depth] = mixed[at]
                out[x, ch * 4 + cls, :, depth : 2 * depth] = grad[at]


def sum_kernel(parts, mixed, grad):
    depth = mixed.shape[1]
    total = parts[0].astype(F32)
    for i in range(1, parts.shape[0]):
        total = total + parts[i].astype(F32)
    mixed[...] = total[:, :depth].astype(BF16)
    grad[...] = total[:, depth:].astype(BF16)


def along_z(x, shift):
    return lax.ppermute(x, Z, [(i, (i + shift) % 16) for i in range(16)])


def swap(x):
    return lax.ppermute(x, "xl", [(0, 1), (1, 0)])


def shards(tokens, grad_out, gate, up, down, gate_scales, up_scales, down_scales):
    n_tok, depth = tokens.shape
    width = gate.shape[1] // 2
    pos = jnp.stack([lax.axis_index("xl"), lax.axis_index("zl")]).astype(jnp.int32)
    both = jnp.stack([tokens, grad_out])
    acts = lax.all_to_all(
        jnp.broadcast_to(both[None], (32,) + both.shape), ("xl",) + TP, 0, 0, tiled=True
    ).reshape(2, 16, 2, n_tok, depth)
    gu_keep, gu_send, d_keep, d_send = call(
        dequant_kernel,
        [((2 * depth, width), BF16)] * 2 + [((width, depth), BF16)] * 2,
        (pos, gate_scales, up_scales, down_scales, gate, up, down),
        "dequant",
        smem=4,
    )
    d_other, gu_other = swap(d_send), swap(gu_send)
    n, all_cols = 4 * n_tok, 3 * width
    plus1, minus1, plus2, minus2, own = call(
        partial_kernel,
        [((n, all_cols), BF16)] * 2 + [((n // 2, all_cols), BF16)] * 2 + [((n, all_cols), F32)],
        (pos, acts, gu_keep, gu_other, d_keep, d_other),
        "partials",
        smem=1,
    )
    a1, b1 = along_z(plus1, 1), along_z(minus1, -1)
    a2, b2 = along_z(plus2, 2), along_z(minus2, -2)
    (window,) = call(window_kernel, [((4, n_tok, all_cols), BF16)], (own, a1, b1, a2, b2), "window")
    (spread,) = call(
        gated_kernel,
        [((4, n_tok, all_cols), BF16)],
        (lax.all_to_all(window, "zh", 0, 0, tiled=True),),
        "gated",
    )
    mine = lax.all_to_all(spread, "zh", 0, 0, tiled=True).reshape(n, all_cols)
    a1, b1 = along_z(mine, 1), along_z(mine, -1)
    a2, b2 = along_z(mine[: n // 2], 2), along_z(mine[n // 2 :], -2)
    (shares,) = call(
        output_kernel,
        [((2, 16, n_tok, 2 * depth), BF16)],
        (pos, mine, a1, b1, a2, b2, gu_keep, gu_other, d_keep, d_other),
        "outputs",
        smem=1,
        scratch=[pltpu.VMEM((4 * n, all_cols), BF16)],
    )
    gathered = lax.all_to_all(
        shares.reshape(32, n_tok, 2 * depth), ("xl",) + TP, 0, 0, tiled=True
    )
    return tuple(
        call(sum_kernel, [((n_tok, depth), BF16)] * 2, (gathered,), "sums")
    )


def solution(mesh):
    fine = Mesh(mesh.devices.reshape(4, 4, 2, 2, 4, 2), ("zh", "zl", "xl", "xh", "y", "core"))
    weights, acts = P(SEQ, TP), P(TP, SEQ)
    return jax.shard_map(
        shards,
        mesh=fine,
        in_specs=(acts, acts, weights, weights, acts, weights, weights, acts),
        out_specs=(acts, acts),
        check_vma=False,
    )
```

time: 647 us -> 179 us (0.28)
  waiting for transfers between devices: 499 us -> 36 us
  starting transfers between devices: 0.21 us -> 58.8 us
  blocking collectives: 101 us -> 68.1 us
  between operations: 13.9 us -> 0.8 us
  matrix products: 9.6 us -> 0 us
  local copies, waits for them, and re-layouts: 15.9 us -> 6.62 us
  Pallas kernels: 0 us -> 7.43 us
    reduce_scatter x4 -> x0, waiting for transfers between devices: 421 us -> none  [the longest x1 145 us: shards(): lax.psum_scatter(jnp.dot(block, w_pair, preferred_element_type=jnp.float3...]
    all_gather x3 -> x0, blocking collectives: 101 us -> none  [the longest x1 53.8 us: shards(): lax.all_gather(hidden, 'seq', axis=0, tiled=True)]
    all_gather x1 -> x0, waiting for transfers between devices: 77.8 us -> none  [shards(): lax.all_gather(joint_grad, 'seq', axis=0, tiled=True)]
    all_to_all x0 -> x3, blocking collectives: none -> 68.1 us  [the longest x1 27 us: shards(): lax.all_to_all(window, 'zh', 0, 0, tiled=True)]
    ppermute x0 -> x10, starting transfers between devices: none -> 50.4 us  [the longest x8 43 us: along_z(): return lax.ppermute(x, Z, [(i, (i + shift) % 16) for i in range(16)])]
    ppermute x0 -> x10, waiting for transfers between devices: none -> 34.5 us  [the longest x2 18.1 us: swap(): return lax.ppermute(x, 'xl', [(0, 1), (1, 0)])]
    dot_general x4 -> x0, matrix products: 9.6 us -> none  [the longest x2 4.77 us: transposed(): lax.dot_general(left, right, (((1,), (1,)), ((), ())), preferred_element_...]
    all_to_all x0 -> x1, starting transfers between devices: none -> 8.39 us  [shards(): lax.all_to_all(jnp.broadcast_to(both[None], (32,) + both.shape), ('xl',)...]
  transfers between devices with their start and end apart: 5 -> 11, of which waited for: 5 -> 6; matrix products, arithmetic and copies ran while one was open for 3% -> 1% of each run, Pallas kernels for 0% -> 0%
where the time goes in v1:
time: 179 us; the launch traced here: 178 us
  blocking collectives  68.1 us (38%)
  starting transfers between devices  58.8 us (33%)
  waiting for transfers between devices  36 us (20%)
  Pallas kernels  7.43 us (4%)
  local copies, waits for them, and re-layouts  6.62 us (4%)
    ppermute x8, starting transfers between devices, along_z(): return lax.ppermute(x, Z, [(i, (i + shift) % 16) for i in range(16)])  43 us
    all_to_all x1, blocking collectives, shards(): lax.all_to_all(window, 'zh', 0, 0, tiled=True)  27 us
    all_to_all x1, blocking collectives, shards(): mine = lax.all_to_all(spread, 'zh', 0, 0, tiled=True).reshape(n, all_cols)  21.8 us
    all_to_all x1, blocking collectives, shards(): lax.all_to_all(shares.reshape(32, n_tok, 2 * depth), ('xl',) + TP, 0, 0,...  19.4 us
    ppermute x2, waiting for transfers between devices, swap(): return lax.ppermute(x, 'xl', [(0, 1), (1, 0)])  18.1 us
    ppermute x8, waiting for transfers between devices, along_z(): return lax.ppermute(x, Z, [(i, (i + shift) % 16) for i in range(16)])  16.4 us
    all_to_all x1, starting transfers between devices, shards(): lax.all_to_all(jnp.broadcast_to(both[None], (32,) + both.shape), ('xl',)...  8.39 us
    pallas_call x6, Pallas kernels, call(): pl.pallas_call(body, out_shape=[jax.ShapeDtypeStruct(s, d) for s, d in ou...  7.43 us
  transfers between devices with their start and end apart: 11, of which 6 were waited for; matrix products, arithmetic and copies ran while one was open for 1% of the time, Pallas kernels for 0%

profile of v1, /device:TPU:1, one launch (start us, length us, event | category | flops | bytes accessed | tf_op | source)
XLA Modules:
  0.0 177.8 jit_solution(6378580290471559259)
XLA Ops:
  2.1 1.2 copy-done
  3.3 1.2 copy-done.1
  5.6 2.1 %dequant.1 = (bf16[512,896]{1,0:T(8,128)(2,1)S(1)}, bf16[512,896]{1,0:T(8,128)(2,1)}, bf16[896,256]{1,0:T(8,128)(2,1)S(1)}, bf16[896,256]{1,0:T(8,128)(2,1)S(1)}) custom-call(s32[2]{0:T(128)S(1)} %pad_add_fusion.pos, f32[2,14]{1,0:T(2,128)S(1)} %copy-done.3, f32[2,14]{1,0:T(2,128)S(1)} %copy-done.4, f32[14,2]{1,0:T(8,128)S(1)} %copy.10.ds, ...), custom_call_target="tpu_custom_call" | custom-call | tf_op jit(solution)/shard_map/dequant/pallas_call | solution.py:21
  8.5 3.9 %collective-permute-start = (bf16[512,896]{1,0:T(8,128)(2,1)}, bf16[512,896]{1,0:T(8,128)(2,1)S(1)}, u32[]{:S(2)}, u32[]{:S(2)}) collective-permute-start(bf16[512,896]{1,0:T(8,128)(2,1)} %get-tuple-element.12), channel_id=1, source_target_pairs={{0,16},{16,0},{1,17},{17,1},{2,18},{18,2},{3,19},{19,3},{4,20},{20... | collective-permute-start | bytes 2752520 | tf_op jit(solution)/shard_map/ppermute | solution.py:155
  13.4 8.4 %all-to-all-start = ((bf16[32,2,16,256]{3,2,1,0:T(8,128)(2,1)}), bf16[32,2,16,256]{3,2,1,0:T(8,128)(2,1)S(1)}, u32[]{:S(2)}, u32[]{:S(2)}) async-start(bf16[32,2,16,256]{3,2,1,0:T(8,128)(2,1)} %broadcast_in_dim.2), calls=%async_computation | async-start | bytes 1048576 | tf_op jit(solution)/shard_map/all_to_all | solution.py:163
  21.8 3.4 %collective-permute-start.1 = (bf16[896,256]{1,0:T(8,128)(2,1)}, bf16[896,256]{1,0:T(8,128)(2,1)S(1)}, u32[]{:S(2)}, u32[]{:S(2)}) collective-permute-start(bf16[896,256]{1,0:T(8,128)(2,1)} %copy-done.5), channel_id=1, source_target_pairs={{0,16},{16,0},{1,17},{17,1},{2,18},{18,2},{3,19},{19,3},{4,20},{20... | collective-permute-start | bytes 1376264 | tf_op jit(solution)/shard_map/ppermute | solution.py:155
  25.2 18.1 %collective-permute-done.1.d_other = bf16[896,256]{1,0:T(8,128)(2,1)S(1)} collective-permute-done((bf16[896,256]{1,0:T(8,128)(2,1)}, bf16[896,256]{1,0:T(8,128)(2,1)S(1)}, u32[]{:S(2)}, u32[]{:S(2)}) %collective-permute-start.1) | collective-permute-done | bytes 458784 | tf_op jit(solution)/shard_map/ppermute | solution.py:155
  43.3 1.5 all-to-all-done
  44.8 2.9 %partials.1 = (bf16[64,2688]{1,0:T(8,128)(2,1)S(1)}, bf16[64,2688]{1,0:T(8,128)(2,1)S(1)}, bf16[32,2688]{1,0:T(8,128)(2,1)S(1)}, bf16[32,2688]{1,0:T(8,128)(2,1)S(1)}, f32[64,2688]{1,0:T(8,128)S(1)}) custom-call(s32[2]{0:T(128)S(1)} %pad_add_fusion.pos, bf16[2,16,2,16,256]{4,3,2,1,0:T(8,128)(2,1)S(1)} %bitcast.13, ...), custom_call_target="tpu_custom_call" | custom-call | tf_op jit(solution)/shard_map/partials/pallas_call | solution.py:21
  47.6 6.9 %collective-permute-start.2 = (bf16[64,2688]{1,0:T(8,128)(2,1)S(1)}, bf16[64,2688]{1,0:T(8,128)(2,1)S(1)}, u32[]{:S(2)}, u32[]{:S(2)}) collective-permute-start(bf16[64,2688]{1,0:T(8,128)(2,1)S(1)} %get-tuple-element.16), channel_id=1, source_target_pairs={{0,32},{32,64},{64,96},{96,128},{128,160},{160,192},{192,224},{224... | collective-permute-start | bytes 1032200 | tf_op jit(solution)/shard_map/ppermute | solution.py:151
  54.6 9.5 %collective-permute-start.3 = (bf16[64,2688]{1,0:T(8,128)(2,1)S(1)}, bf16[64,2688]{1,0:T(8,128)(2,1)S(1)}, u32[]{:S(2)}, u32[]{:S(2)}) collective-permute-start(bf16[64,2688]{1,0:T(8,128)(2,1)S(1)} %get-tuple-element.17), channel_id=1, source_target_pairs={{0,480},{32,0},{64,32},{96,64},{128,96},{160,128},{192,160},{224,1... | collective-permute-start | bytes 1032200 | tf_op jit(solution)/shard_map/ppermute | solution.py:151
  64.1 1.9 %collective-permute-start.4 = (bf16[32,2688]{1,0:T(8,128)(2,1)S(1)}, bf16[32,2688]{1,0:T(8,128)(2,1)S(1)}, u32[]{:S(2)}, u32[]{:S(2)}) collective-permute-start(bf16[32,2688]{1,0:T(8,128)(2,1)S(1)} %get-tuple-element.18), channel_id=1, source_target_pairs={{0,64},{32,96},{64,128},{96,160},{128,192},{160,224},{192,256},{22... | collective-permute-start | bytes 516104 | tf_op jit(solution)/shard_map/ppermute | solution.py:151
  66.0 5.5 %collective-permute-start.5 = (bf16[32,2688]{1,0:T(8,128)(2,1)S(1)}, bf16[32,2688]{1,0:T(8,128)(2,1)S(1)}, u32[]{:S(2)}, u32[]{:S(2)}) collective-permute-start(bf16[32,2688]{1,0:T(8,128)(2,1)S(1)} %get-tuple-element.19), channel_id=1, source_target_pairs={{0,448},{32,480},{64,0},{96,32},{128,64},{160,96},{192,128},{224,1... | collective-permute-start | bytes 516104 | tf_op jit(solution)/shard_map/ppermute | solution.py:151
  71.5 4.9 %collective-permute-done.4.a2 = bf16[32,2688]{1,0:T(8,128)(2,1)S(1)} collective-permute-done((bf16[32,2688]{1,0:T(8,128)(2,1)S(1)}, bf16[32,2688]{1,0:T(8,128)(2,1)S(1)}, u32[]{:S(2)}, u32[]{:S(2)}) %collective-permute-start.4) | collective-permute-done | bytes 172064 | tf_op jit(solution)/shard_map/ppermute | solution.py:151
  77.5 27.0 %all_to_all.20.parts = bf16[4,16,2688]{2,1,0:T(8,128)(2,1)S(1)} all-to-all(bf16[4,16,2688]{2,1,0:T(8,128)(2,1)S(1)} %window.1), channel_id=1, replica_groups=mesh['zh'=4,'zl'=4,'xl'=2,'xh'=2,'y'=4,'core'=2] {'zh'}, dimensions={0} | all-to-all | bytes 688128 | tf_op jit(solution)/shard_map/all_to_all | solution.py:188
  104.6 21.8 %all_to_all.21 = bf16[4,16,2688]{2,1,0:T(8,128)(2,1)S(1)} all-to-all(bf16[4,16,2688]{2,1,0:T(8,128)(2,1)S(1)} %gated.1), channel_id=1, replica_groups=mesh['zh'=4,'zl'=4,'xl'=2,'xh'=2,'y'=4,'core'=2] {'zh'}, dimensions={0} | all-to-all | bytes 688128 | tf_op jit(solution)/shard_map/all_to_all | solution.py:191
  126.4 1.9 %collective-permute-start.7 = (bf16[64,2688]{1,0:T(8,128)(2,1)S(1)}, bf16[64,2688]{1,0:T(8,128)(2,1)S(1)}, u32[]{:S(2)}, u32[]{:S(2)}) collective-permute-start(bf16[64,2688]{1,0:T(8,128)(2,1)S(1)} %bitcast.9), channel_id=1, source_target_pairs={{0,480},{32,0},{64,32},{96,64},{128,96},{160,128},{192,160},{224,1... | collective-permute-start | bytes 1032200 | tf_op jit(solution)/shard_map/ppermute | solution.py:151
  128.3 3.4 %collective-permute-start.6 = (bf16[64,2688]{1,0:T(8,128)(2,1)S(1)}, bf16[64,2688]{1,0:T(8,128)(2,1)S(1)}, u32[]{:S(2)}, u32[]{:S(2)}) collective-permute-start(bf16[64,2688]{1,0:T(8,128)(2,1)S(1)} %bitcast.10), channel_id=1, source_target_pairs={{0,32},{32,64},{64,96},{96,128},{128,160},{160,192},{192,224},{224... | collective-permute-start | bytes 1032200 | tf_op jit(solution)/shard_map/ppermute | solution.py:151
  131.7 12.0 %collective-permute-start.8 = (bf16[32,2688]{1,0:T(8,128)(2,1)S(1)}, bf16[32,2688]{1,0:T(8,128)(2,1)S(1)}, u32[]{:S(2)}, u32[]{:S(2)}) collective-permute-start(bf16[32,2688]{1,0:T(8,128)(2,1)S(1)} %bitcast.15), channel_id=1, source_target_pairs={{0,64},{32,96},{64,128},{96,160},{128,192},{160,224},{192,256},{22... | collective-permute-start | bytes 516104 | tf_op jit(solution)/shard_map/ppermute | solution.py:151
  143.7 1.9 %collective-permute-start.9 = (bf16[32,2688]{1,0:T(8,128)(2,1)S(1)}, bf16[32,2688]{1,0:T(8,128)(2,1)S(1)}, u32[]{:S(2)}, u32[]{:S(2)}) collective-permute-start(bf16[32,2688]{1,0:T(8,128)(2,1)S(1)} %bitcast.14), channel_id=1, source_target_pairs={{0,448},{32,480},{64,0},{96,32},{128,64},{160,96},{192,128},{224,1... | collective-permute-start | bytes 516104 | tf_op jit(solution)/shard_map/ppermute | solution.py:151
  145.7 5.7 %collective-permute-done.8.a2 = bf16[32,2688]{1,0:T(8,128)(2,1)S(1)} collective-permute-done((bf16[32,2688]{1,0:T(8,128)(2,1)S(1)}, bf16[32,2688]{1,0:T(8,128)(2,1)S(1)}, u32[]{:S(2)}, u32[]{:S(2)}) %collective-permute-start.8) | collective-permute-done | bytes 172064 | tf_op jit(solution)/shard_map/ppermute | solution.py:151
  151.3 4.8 %collective-permute-done.9.b2 = bf16[32,2688]{1,0:T(8,128)(2,1)S(1)} collective-permute-done((bf16[32,2688]{1,0:T(8,128)(2,1)S(1)}, bf16[32,2688]{1,0:T(8,128)(2,1)S(1)}, u32[]{:S(2)}, u32[]{:S(2)}) %collective-permute-start.9) | collective-permute-done | bytes 172064 | tf_op jit(solution)/shard_map/ppermute | solution.py:151
  156.2 1.5 outputs.1
  157.7 19.4 %all_to_all.22.parts = bf16[32,16,512]{2,1,0:T(8,128)(2,1)S(1)} all-to-all(bf16[32,16,512]{2,1,0:T(8,128)(2,1)S(1)} %bitcast.12), channel_id=1, replica_groups=mesh['zh'=4,'zl'=4,'xl'=2,'xh'=2,'y'=4,'core'=2] {'xl','xh','y','core'}, dimensions={0} | all-to-all | bytes 1048576 | tf_op jit(solution)/shard_map/all_to_all | solution.py:202
  (30 shorter events, 6.2 us)
Async XLA Ops:
  0.6 0.7 copy-start.8
  1.4 0.7 copy-start.4
  1.4 0.7 copy-start.3
  2.1 1.2 copy-start
  3.3 1.2 copy-start.1
  4.5 1.2 copy-start.2
  5.6 6.8 %copy-start.6 = (bf16[16,256]{1,0:T(8,128)(2,1)S(1)}, bf16[16,256]{1,0:T(8,128)(2,1)}, u32[]{:S(2)}) copy-start(bf16[16,256]{1,0:T(8,128)(2,1)} %param.9) | copy-start | bytes 24580
  5.6 6.8 %copy-start.7 = (bf16[16,256]{1,0:T(8,128)(2,1)S(1)}, bf16[16,256]{1,0:T(8,128)(2,1)}, u32[]{:S(2)}) copy-start(bf16[16,256]{1,0:T(8,128)(2,1)} %param.8) | copy-start | bytes 24580
  7.8 0.8 copy-start.5
  8.5 36.2 %collective-permute-start = (bf16[512,896]{1,0:T(8,128)(2,1)}, bf16[512,896]{1,0:T(8,128)(2,1)S(1)}, u32[]{:S(2)}, u32[]{:S(2)}) collective-permute-start(bf16[512,896]{1,0:T(8,128)(2,1)} %get-tuple-element.12), channel_id=1, source_target_pairs={{0,16},{16,0},{1,17},{17,1},{2,18},{18,2},{3,19},{19,3},{4,20},{20... | collective-permute-start | bytes 2752520 | tf_op jit(solution)/shard_map/ppermute | solution.py:155
  13.4 31.4 %all-to-all-start = ((bf16[32,2,16,256]{3,2,1,0:T(8,128)(2,1)}), bf16[32,2,16,256]{3,2,1,0:T(8,128)(2,1)S(1)}, u32[]{:S(2)}, u32[]{:S(2)}) async-start(bf16[32,2,16,256]{3,2,1,0:T(8,128)(2,1)} %broadcast_in_dim.2), calls=%async_computation | async-start | bytes 1048576 | tf_op jit(solution)/shard_map/all_to_all | solution.py:163
  21.8 21.5 %collective-permute-start.1 = (bf16[896,256]{1,0:T(8,128)(2,1)}, bf16[896,256]{1,0:T(8,128)(2,1)S(1)}, u32[]{:S(2)}, u32[]{:S(2)}) collective-permute-start(bf16[896,256]{1,0:T(8,128)(2,1)} %copy-done.5), channel_id=1, source_target_pairs={{0,16},{16,0},{1,17},{17,1},{2,18},{18,2},{3,19},{19,3},{4,20},{20... | collective-permute-start | bytes 1376264 | tf_op jit(solution)/shard_map/ppermute | solution.py:155
  47.6 29.7 %collective-permute-start.2 = (bf16[64,2688]{1,0:T(8,128)(2,1)S(1)}, bf16[64,2688]{1,0:T(8,128)(2,1)S(1)}, u32[]{:S(2)}, u32[]{:S(2)}) collective-permute-start(bf16[64,2688]{1,0:T(8,128)(2,1)S(1)} %get-tuple-element.16), channel_id=1, source_target_pairs={{0,32},{32,64},{64,96},{96,128},{128,160},{160,192},{192,224},{224... | collective-permute-start | bytes 1032200 | tf_op jit(solution)/shard_map/ppermute | solution.py:151
  54.6 22.8 %collective-permute-start.3 = (bf16[64,2688]{1,0:T(8,128)(2,1)S(1)}, bf16[64,2688]{1,0:T(8,128)(2,1)S(1)}, u32[]{:S(2)}, u32[]{:S(2)}) collective-permute-start(bf16[64,2688]{1,0:T(8,128)(2,1)S(1)} %get-tuple-element.17), channel_id=1, source_target_pairs={{0,480},{32,0},{64,32},{96,64},{128,96},{160,128},{192,160},{224,1... | collective-permute-start | bytes 1032200 | tf_op jit(solution)/shard_map/ppermute | solution.py:151
  64.1 12.3 %collective-permute-start.4 = (bf16[32,2688]{1,0:T(8,128)(2,1)S(1)}, bf16[32,2688]{1,0:T(8,128)(2,1)S(1)}, u32[]{:S(2)}, u32[]{:S(2)}) collective-permute-start(bf16[32,2688]{1,0:T(8,128)(2,1)S(1)} %get-tuple-element.18), channel_id=1, source_target_pairs={{0,64},{32,96},{64,128},{96,160},{128,192},{160,224},{192,256},{22... | collective-permute-start | bytes 516104 | tf_op jit(solution)/shard_map/ppermute | solution.py:151
  66.0 11.4 %collective-permute-start.5 = (bf16[32,2688]{1,0:T(8,128)(2,1)S(1)}, bf16[32,2688]{1,0:T(8,128)(2,1)S(1)}, u32[]{:S(2)}, u32[]{:S(2)}) collective-permute-start(bf16[32,2688]{1,0:T(8,128)(2,1)S(1)} %get-tuple-element.19), channel_id=1, source_target_pairs={{0,448},{32,480},{64,0},{96,32},{128,64},{160,96},{192,128},{224,1... | collective-permute-start | bytes 516104 | tf_op jit(solution)/shard_map/ppermute | solution.py:151
  126.4 29.8 %collective-permute-start.7 = (bf16[64,2688]{1,0:T(8,128)(2,1)S(1)}, bf16[64,2688]{1,0:T(8,128)(2,1)S(1)}, u32[]{:S(2)}, u32[]{:S(2)}) collective-permute-start(bf16[64,2688]{1,0:T(8,128)(2,1)S(1)} %bitcast.9), channel_id=1, source_target_pairs={{0,480},{32,0},{64,32},{96,64},{128,96},{160,128},{192,160},{224,1... | collective-permute-start | bytes 1032200 | tf_op jit(solution)/shard_map/ppermute | solution.py:151
  128.3 27.9 %collective-permute-start.6 = (bf16[64,2688]{1,0:T(8,128)(2,1)S(1)}, bf16[64,2688]{1,0:T(8,128)(2,1)S(1)}, u32[]{:S(2)}, u32[]{:S(2)}) collective-permute-start(bf16[64,2688]{1,0:T(8,128)(2,1)S(1)} %bitcast.10), channel_id=1, source_target_pairs={{0,32},{32,64},{64,96},{96,128},{128,160},{160,192},{192,224},{224... | collective-permute-start | bytes 1032200 | tf_op jit(solution)/shard_map/ppermute | solution.py:151
  131.7 19.6 %collective-permute-start.8 = (bf16[32,2688]{1,0:T(8,128)(2,1)S(1)}, bf16[32,2688]{1,0:T(8,128)(2,1)S(1)}, u32[]{:S(2)}, u32[]{:S(2)}) collective-permute-start(bf16[32,2688]{1,0:T(8,128)(2,1)S(1)} %bitcast.15), channel_id=1, source_target_pairs={{0,64},{32,96},{64,128},{96,160},{128,192},{160,224},{192,256},{22... | collective-permute-start | bytes 516104 | tf_op jit(solution)/shard_map/ppermute | solution.py:151
  143.7 12.4 %collective-permute-start.9 = (bf16[32,2688]{1,0:T(8,128)(2,1)S(1)}, bf16[32,2688]{1,0:T(8,128)(2,1)S(1)}, u32[]{:S(2)}, u32[]{:S(2)}) collective-permute-start(bf16[32,2688]{1,0:T(8,128)(2,1)S(1)} %bitcast.14), channel_id=1, source_target_pairs={{0,448},{32,480},{64,0},{96,32},{128,64},{160,96},{192,128},{224,1... | collective-permute-start | bytes 516104 | tf_op jit(solution)/shard_map/ppermute | solution.py:151

commit v2 on v0

v2 whole, which is shorter than its diff:
```python
import functools

import jax
import jax.numpy as jnp
from jax import lax
from jax.experimental import pallas as pl
from jax.experimental.pallas import tpu as pltpu
from jax.sharding import Mesh, PartitionSpec as P

BLK = 128
Z = ("zh", "zl")
TP = ("xh", "y", "core")
SEQ = ("zh", "zl", "xl")
F32, BF16 = jnp.float32, jnp.bfloat16
VMEM = pl.BlockSpec(memory_space=pltpu.VMEM)
SMEM = pl.BlockSpec(memory_space=pltpu.SMEM)
ANY = pl.BlockSpec(memory_space=pl.ANY)


def call(body, out_shapes, ins, name, specs=None, scratch=(), limit=16):
    return pl.pallas_call(
        body,
        out_shape=[jax.ShapeDtypeStruct(s, d) for s, d in out_shapes],
        in_specs=specs or [VMEM] * len(ins),
        out_specs=[VMEM] * len(out_shapes),
        scratch_shapes=list(scratch),
        compiler_params=pltpu.CompilerParams(vmem_limit_bytes=limit * 1024 * 1024),
        name=name,
    )(*ins)


def scale_kernel(kept, chunks, repeats, *refs):
    scales, (gate, up, down) = refs[:3], refs[3:6]
    outs, (g_buf, u_buf, d_buf), tables = refs[6:-7], refs[-7:-4], refs[-4:-1]
    sems = refs[-1]
    depth = g_buf.shape[0]
    half = gate.shape[1] // (2 * BLK)
    xl = lax.axis_index("xl")
    start = (xl if kept else 1 - xl) * half
    lo, count = chunks[0][0], sum(c for _, c in chunks)
    at = pl.ds(pl.multiple_of((start + lo) * BLK, BLK), count * BLK)
    pairs = [(down.at[at, :], d_buf), (gate.at[:, at], g_buf), (up.at[:, at], u_buf)]
    pairs = list(zip(scales, tables)) + pairs
    copies = [pltpu.make_async_copy(a, b, sems.at[i]) for i, (a, b) in enumerate(pairs)]
    for copy in copies[3:] + copies[:3]:
        copy.start()
    for copy in copies[:3]:
        copy.wait()
    gs, us, ds = tables
    for which, copy in enumerate(copies[3:]):
        copy.wait()
        for (first, n), *out in zip(chunks, *(outs[r * len(chunks) :] for r in range(repeats))):
            for j in range(first, first + n):
                src = slice((j - lo) * BLK, (j - lo + 1) * BLK)
                cols = slice((j - first) * BLK, (j - first + 1) * BLK)
                for i in range(depth // BLK):
                    rows = slice(i * BLK, (i + 1) * BLK)
                    if which == 0:
                        to = slice(2 * depth + i * BLK, 2 * depth + (i + 1) * BLK)
                        value = (d_buf[src, rows].astype(F32) * ds[i, start + j]).T
                    elif which == 1:
                        to = rows
                        value = g_buf[rows, src].astype(F32) * gs[i, start + j]
                    else:
                        to = slice(depth + i * BLK, depth + (i + 1) * BLK)
                        value = u_buf[rows, src].astype(F32) * us[i, start + j]
                    for ref in out:
                        ref[to, cols] = value.astype(BF16)


def nt(a, b):
    return lax.dot_general(a, b, (((1,), (1,)), ((), ())), preferred_element_type=F32)


def nn(a, b):
    return jnp.dot(a, b, preferred_element_type=F32)


def toward():
    return 1 - 2 * lax.axis_index("core")


def partial_kernel(width, acts, keep_in, other_in, *refs):
    ahead, behind, far, own, keep, other, sems = refs[-7:]
    copies = [
        pltpu.make_async_copy(keep_in, keep, sems.at[0]),
        pltpu.make_async_copy(other_in, other, sems.at[1]),
    ]
    for copy in copies:
        copy.start()
    for copy in copies:
        copy.wait()
    xl, zl, turn = lax.axis_index("xl"), lax.axis_index("zl"), toward()
    depth = keep.shape[0] // 3
    for shift, out in ((turn, ahead), (-turn, behind), (2, far), (0, own)):
        cls = lax.rem(zl + shift + 4, 4)

        def rows(x, which):
            return jnp.concatenate([acts[x, ch * 4 + cls, which] for ch in range(4)], axis=0)

        for which, ks in ((0, (0, 1)), (1, (2,))):
            mine, his = rows(xl, which), rows(1 - xl, which)
            for k in ks:
                w = slice(k * depth, (k + 1) * depth)
                part = nn(mine, keep[w]) + nn(his, other[w])
                out[:, k * width : (k + 1) * width] = part.astype(out.dtype)


def window_kernel(*refs):
    out, left = refs[-1], 0
    n = out.shape[1]
    for k in range(0, len(refs) - 1, 4):
        own, *parts = refs[k : k + 4]
        width = own.shape[1]
        for i in range(out.shape[0]):
            rows = slice(i * n, (i + 1) * n)
            total = own[rows, :]
            for part in parts:
                total = total + part[rows, :].astype(F32)
            out[i, :, left : left + width] = total.astype(BF16)
        left += width


def spans(widths):
    left, at = 0, []
    for w in widths:
        at.append([slice(left + k * w, left + (k + 1) * w) for k in range(3)])
        left += 3 * w
    return at


def gated_kernel(widths, parts, out):
    def total(cols):
        s = parts[0, :, cols].astype(F32)
        for i in range(1, parts.shape[0]):
            s = s + parts[i, :, cols].astype(F32)
        return s

    for at in spans(widths):
        gate_sum, up_sum, back_sum = (total(cols) for cols in at)
        sig = jax.nn.sigmoid(gate_sum)
        active = gate_sum * sig
        results = (
            active * up_sum,
            back_sum * up_sum * (sig * (1.0 + gate_sum * (1.0 - sig))),
            back_sum * active,
        )
        for cols, result in zip(at, results):
            for i in range(out.shape[0]):
                out[i, :, cols] = result.astype(BF16)


def output_kernel(widths, own, ahead, behind, far, *refs):
    weights, out, rows = refs[:-2], refs[-2], refs[-1]
    xl, zl, turn = lax.axis_index("xl"), lax.axis_index("zl"), toward()
    n = out.shape[1] // 16
    depth = weights[0].shape[0] // 3
    for shift, src in ((0, own), (-turn, ahead), (turn, behind), (2, far)):
        cls = lax.rem(zl + shift + 4, 4)
        for i in range(4):
            at = pl.ds(pl.multiple_of((i * 4 + cls) * n, n), n)
            rows[at, :] = src[i * n : (i + 1) * n, :]
    for k, x in enumerate((xl, 1 - xl)):
        mixed = grad = 0.0
        for c, at in enumerate(spans(widths)):
            w = weights[2 * c + k]
            hidden, gate_grad, up_grad = (rows[:, cols] for cols in at)
            mixed = mixed + nt(hidden, w[2 * depth :])
            grad = grad + nt(gate_grad, w[:depth]) + nt(up_grad, w[depth : 2 * depth])
        out[x, :, 0:depth] = mixed.astype(BF16)
        out[x, :, depth : 2 * depth] = grad.astype(BF16)


def sum_kernel(parts, mixed, grad):
    depth = mixed.shape[1]
    total = parts[0].astype(F32)
    for i in range(1, parts.shape[0]):
        total = total + parts[i].astype(F32)
    mixed[...] = total[:, :depth].astype(BF16)
    grad[...] = total[:, depth:].astype(BF16)


def along_z(x, shift):
    pairs = [(2 * z + c, 2 * ((z + shift * (1 - 2 * c)) % 16) + c) for z in range(16) for c in range(2)]
    return lax.ppermute(x, Z + ("core",), pairs)


def exchange(x):
    return tuple(along_z(x[i], shift) for i, shift in enumerate((1, -1, 2)))


def shards(tokens, grad_out, gate, up, down, gate_scales, up_scales, down_scales):
    n_tok, depth = tokens.shape
    half = gate.shape[1] // (2 * BLK)
    chunks = ((0, (half + 1) // 2), ((half + 1) // 2, half // 2))

    def scaled(kept, chunks, limit, copies=1):
        w = sum(count for _, count in chunks) * BLK
        outs = call(
            functools.partial(scale_kernel, kept, chunks, copies),
            [((3 * depth, count * BLK), BF16) for _, count in chunks] * copies,
            (gate_scales, up_scales, down_scales.T, gate, up, down),
            "scaled",
            specs=[ANY] * 6,
            scratch=[pltpu.VMEM((depth, w), BF16)] * 2
            + [pltpu.VMEM((w, depth), BF16)]
            + [pltpu.SMEM(gate_scales.shape, F32)] * 3
            + [pltpu.SemaphoreType.DMA((6,))],
            limit=limit,
        )
        return outs[: len(chunks)], outs[len(chunks) :]

    def swap(x):
        return lax.ppermute(x, "xl", [(0, 1), (1, 0)])

    (first, second), _ = scaled(False, chunks, 60)
    keeps, _ = scaled(True, chunks, 60)
    first_other = swap(first)
    second, tokens, grad_out = lax.optimization_barrier((second, tokens, grad_out))
    acts = jnp.stack([tokens, grad_out])
    acts = lax.all_to_all(
        jnp.broadcast_to(acts[None], (32,) + acts.shape), ("xl",) + TP, 0, 0, tiled=True
    ).reshape(2, 16, 2, n_tok, depth)
    first_other, second, keeps = lax.optimization_barrier((first_other, second, keeps))
    others = (first_other, swap(second))

    n = 4 * n_tok
    widths = tuple(count * BLK for _, count in chunks)
    w = 3 * sum(widths)
    weights, windows = [], []
    for keep, other, width in zip(keeps, others, widths):
        ins = (acts, keep, other, *windows[1:2])
        *parts, own = call(
            functools.partial(partial_kernel, width),
            [((n, 3 * width), BF16)] * 3 + [((n, 3 * width), F32)],
            ins,
            "partials",
            specs=[VMEM] + [ANY] * (len(ins) - 1),
            scratch=[pltpu.VMEM(keep.shape, BF16)] * 2 + [pltpu.SemaphoreType.DMA((2,))],
        )
        windows += [own, *exchange(parts)]
        weights += [keep, other]
    (window,) = call(window_kernel, [((4, n_tok, w), BF16)], windows, "window")
    (spread,) = call(
        functools.partial(gated_kernel, widths),
        [((4, n_tok, w), BF16)],
        (lax.all_to_all(window, "zh", 0, 0, tiled=True),),
        "gated",
    )
    mine = lax.all_to_all(spread, "zh", 0, 0, tiled=True).reshape(n, w)
    (shares,) = call(
        functools.partial(output_kernel, widths),
        [((2, 16 * n_tok, 2 * depth), BF16)],
        (mine, *exchange([mine] * 3), *weights),
        "outputs",
        scratch=[pltpu.VMEM((4 * n, w), BF16)],
    )
    gathered = lax.all_to_all(
        shares.reshape(32, n_tok, 2 * depth), ("xl",) + TP, 0, 0, tiled=True
    )
    return tuple(call(sum_kernel, [((n_tok, depth), BF16)] * 2, (gathered,), "sums"))


def solution(mesh):
    fine = Mesh(mesh.devices.reshape(4, 4, 2, 2, 4, 2), ("zh", "zl", "xl", "xh", "y", "core"))
    weights, acts = P(SEQ, TP), P(TP, SEQ)
    return jax.shard_map(
        shards,
        mesh=fine,
        in_specs=(acts, acts, weights, weights, acts, weights, weights, acts),
        out_specs=(acts, acts),
        check_vma=False,
    )
```

time: 647 us -> 165 us (0.26)
  waiting for transfers between devices: 499 us -> 29.2 us
  starting transfers between devices: 0.21 us -> 51.6 us
  blocking collectives: 101 us -> 70.7 us
  local copies, waits for them, and re-layouts: 15.9 us -> 2 us
  between operations: 13.9 us -> 0.88 us
  matrix products: 9.6 us -> 0 us
  Pallas kernels: 0 us -> 9.5 us
    reduce_scatter x4 -> x0, waiting for transfers between devices: 421 us -> none  [the longest x1 145 us: shards(): lax.psum_scatter(jnp.dot(block, w_pair, preferred_element_type=jnp.float3...]
    all_gather x3 -> x0, blocking collectives: 101 us -> none  [the longest x1 53.8 us: shards(): lax.all_gather(hidden, 'seq', axis=0, tiled=True)]
    all_gather x1 -> x0, waiting for transfers between devices: 77.8 us -> none  [shards(): lax.all_gather(joint_grad, 'seq', axis=0, tiled=True)]
    all_to_all x0 -> x3, blocking collectives: none -> 70.7 us  [the longest x1 26.5 us: shards(): lax.all_to_all(window, 'zh', 0, 0, tiled=True)]
    ppermute x0 -> x11, starting transfers between devices: none -> 43.3 us  [the longest x9 35.3 us: along_z(): return lax.ppermute(x, Z + ('core',), pairs)]
    ppermute x0 -> x11, waiting for transfers between devices: none -> 16.3 us  [the longest x9 15.6 us: along_z(): return lax.ppermute(x, Z + ('core',), pairs)]
    all_to_all x0 -> x1, waiting for transfers between devices: none -> 12.9 us  [shards(): lax.all_to_all(jnp.broadcast_to(acts[None], (32,) + acts.shape), ('xl',)...]
    unnamed x25 -> x12, local copies, waits for them, and re-layouts: 13.7 us -> 1.15 us
  transfers between devices with their start and end apart: 5 -> 12, of which waited for: 5 -> 6; matrix products, arithmetic and copies ran while one was open for 3% -> 1% of each run, Pallas kernels for 0% -> 3%
where the time goes in v2:
time: 165 us; the launch traced here: 164 us
  blocking collectives  70.7 us (43%)
  starting transfers between devices  51.6 us (31%)
  waiting for transfers between devices  29.2 us (18%)
  Pallas kernels  9.5 us (6%)
  local copies, waits for them, and re-layouts  2 us (1%)
    ppermute x9, starting transfers between devices, along_z(): return lax.ppermute(x, Z + ('core',), pairs)  35.3 us
    all_to_all x1, blocking collectives, shards(): lax.all_to_all(window, 'zh', 0, 0, tiled=True)  26.5 us
    all_to_all x1, blocking collectives, shards(): mine = lax.all_to_all(spread, 'zh', 0, 0, tiled=True).reshape(n, w)  26.2 us
    all_to_all x1, blocking collectives, shards(): lax.all_to_all(shares.reshape(32, n_tok, 2 * depth), ('xl',) + TP, 0, 0,...  18.1 us
    ppermute x9, waiting for transfers between devices, along_z(): return lax.ppermute(x, Z + ('core',), pairs)  15.6 us
    all_to_all x1, waiting for transfers between devices, shards(): lax.all_to_all(jnp.broadcast_to(acts[None], (32,) + acts.shape), ('xl',)...  12.9 us
    pallas_call x8, Pallas kernels, call(): pl.pallas_call(body, out_shape=[jax.ShapeDtypeStruct(s, d) for s, d in ou...  9.5 us
    all_to_all x1, starting transfers between devices, shards(): lax.all_to_all(jnp.broadcast_to(acts[None], (32,) + acts.shape), ('xl',)...  8.39 us
  transfers between devices with their start and end apart: 12, of which 6 were waited for; matrix products, arithmetic and copies ran while one was open for 1% of the time, Pallas kernels for 3%

profile of v2, /device:TPU:1, one launch (start us, length us, event | category | flops | bytes accessed | tf_op | source)
XLA Modules:
  0.0 163.9 jit_solution(13869424495492292613)
XLA Ops:
  0.6 2.6 %scaled.2 = (bf16[768,512]{1,0:T(8,128)(2,1)}, bf16[768,384]{1,0:T(8,128)(2,1)}) custom-call(f32[2,14]{1,0:T(2,128)} %refs_0_.3, f32[2,14]{1,0:T(2,128)} %refs_1_.3, f32[2,14]{1,0:T(2,128)} %bitcast.15, bf16[256,1792]{1,0:T(8,128)(2,1)} %refs_3_.3, bf16[256,1792]{1,0:T(8,128)(2,1)} %refs_4_.3, bf16[1792,256]{1,0:T(8,128)(2,1)} %refs_5_.3), custom_call_target="tpu_custom_call" | custom-call | tf_op jit(solution)/shard_map/scaled/pallas_call | solution.py:21
  3.2 3.9 %collective-permute-start = (bf16[768,512]{1,0:T(8,128)(2,1)}, bf16[768,512]{1,0:T(8,128)(2,1)S(1)}, u32[]{:S(2)}, u32[]{:S(2)}) collective-permute-start(bf16[768,512]{1,0:T(8,128)(2,1)} %get-tuple-element.24), channel_id=1, source_target_pairs={{0,16},{16,0},{1,17},{17,1},{2,18},{18,2},{3,19},{19,3},{4,20},{20... | collective-permute-start | bytes 2359304 | tf_op jit(solution)/shard_map/ppermute | solution.py:214
  8.1 8.4 %all-to-all-start = ((bf16[32,2,16,256]{3,2,1,0:T(8,128)(2,1)}), bf16[32,2,16,256]{3,2,1,0:T(8,128)(2,1)S(1)}, u32[]{:S(2)}, u32[]{:S(2)}) async-start(bf16[32,2,16,256]{3,2,1,0:T(8,128)(2,1)} %broadcast_in_dim.2), calls=%async_computation | async-start | bytes 1048576 | tf_op jit(solution)/shard_map/all_to_all | solution.py:221
  16.5 2.6 %scaled.3 = (bf16[768,512]{1,0:T(8,128)(2,1)}, bf16[768,384]{1,0:T(8,128)(2,1)}) custom-call(f32[2,14]{1,0:T(2,128)} %refs_0_.3, f32[2,14]{1,0:T(2,128)} %refs_1_.3, f32[2,14]{1,0:T(2,128)} %bitcast.16, bf16[256,1792]{1,0:T(8,128)(2,1)} %refs_3_.3, bf16[256,1792]{1,0:T(8,128)(2,1)} %refs_4_.3, bf16[1792,256]{1,0:T(8,128)(2,1)} %refs_5_.3), custom_call_target="tpu_custom_call" | custom-call | tf_op jit(solution)/shard_map/scaled/pallas_call | solution.py:21
  19.7 4.0 %collective-permute-start.4 = (bf16[768,384]{1,0:T(8,128)(2,1)S(1)}, bf16[768,384]{1,0:T(8,128)(2,1)S(1)}, u32[]{:S(2)}, u32[]{:S(2)}) collective-permute-start(bf16[768,384]{1,0:T(8,128)(2,1)S(1)} %copy-done.5), channel_id=1, source_target_pairs={{0,16},{16,0},{1,17},{17,1},{2,18},{18,2},{3,19},{19,3},{4,20},{20... | collective-permute-start | bytes 1769480 | tf_op jit(solution)/shard_map/ppermute | solution.py:214
  23.7 12.9 %all-to-all-done = bf16[32,2,16,256]{3,2,1,0:T(8,128)(2,1)S(1)} async-done(((bf16[32,2,16,256]{3,2,1,0:T(8,128)(2,1)}), bf16[32,2,16,256]{3,2,1,0:T(8,128)(2,1)S(1)}, u32[]{:S(2)}, u32[]{:S(2)}) %all-to-all-start) | async-done | bytes 524320 | tf_op jit(solution)/shard_map/all_to_all | solution.py:221
  36.7 1.1 copy-done
  37.8 1.3 partials.2
  39.1 11.1 %collective-permute-start.1 = (bf16[64,1536]{1,0:T(8,128)(2,1)S(1)}, bf16[64,1536]{1,0:T(8,128)(2,1)S(1)}, u32[]{:S(2)}, u32[]{:S(2)}) collective-permute-start(bf16[64,1536]{1,0:T(8,128)(2,1)S(1)} %get-tuple-element.31), channel_id=1, source_target_pairs={{0,32},{1,481},{32,64},{33,1},{64,96},{65,33},{96,128},{97,65},{12... | collective-permute-start | bytes 589832 | tf_op jit(solution)/shard_map/ppermute | solution.py:185
  50.3 1.9 %collective-permute-start.2 = (bf16[64,1536]{1,0:T(8,128)(2,1)S(1)}, bf16[64,1536]{1,0:T(8,128)(2,1)S(1)}, u32[]{:S(2)}, u32[]{:S(2)}) collective-permute-start(bf16[64,1536]{1,0:T(8,128)(2,1)S(1)} %get-tuple-element.32), channel_id=1, source_target_pairs={{0,480},{1,33},{32,0},{33,65},{64,32},{65,97},{96,64},{97,129},{12... | collective-permute-start | bytes 589832 | tf_op jit(solution)/shard_map/ppermute | solution.py:185
  52.2 3.8 %collective-permute-start.3 = (bf16[64,1536]{1,0:T(8,128)(2,1)S(1)}, bf16[64,1536]{1,0:T(8,128)(2,1)S(1)}, u32[]{:S(2)}, u32[]{:S(2)}) collective-permute-start(bf16[64,1536]{1,0:T(8,128)(2,1)S(1)} %get-tuple-element.33), channel_id=1, source_target_pairs={{0,64},{1,449},{32,96},{33,481},{64,128},{65,1},{96,160},{97,33},{... | collective-permute-start | bytes 589832 | tf_op jit(solution)/shard_map/ppermute | solution.py:185
  57.2 2.7 %collective-permute-start.5 = (bf16[64,1152]{1,0:T(8,128)(2,1)S(1)}, bf16[64,1152]{1,0:T(8,128)(2,1)S(1)}, u32[]{:S(2)}, u32[]{:S(2)}) collective-permute-start(bf16[64,1152]{1,0:T(8,128)(2,1)S(1)} %get-tuple-element.37), channel_id=1, source_target_pairs={{0,32},{1,481},{32,64},{33,1},{64,96},{65,33},{96,128},{97,65},{12... | collective-permute-start | bytes 442376 | tf_op jit(solution)/shard_map/ppermute | solution.py:185
  59.8 3.1 %collective-permute-start.6 = (bf16[64,1152]{1,0:T(8,128)(2,1)S(1)}, bf16[64,1152]{1,0:T(8,128)(2,1)S(1)}, u32[]{:S(2)}, u32[]{:S(2)}) collective-permute-start(bf16[64,1152]{1,0:T(8,128)(2,1)S(1)} %get-tuple-element.38), channel_id=1, source_target_pairs={{0,480},{1,33},{32,0},{33,65},{64,32},{65,97},{96,64},{97,129},{12... | collective-permute-start | bytes 442376 | tf_op jit(solution)/shard_map/ppermute | solution.py:185
  62.9 4.3 %collective-permute-start.7 = (bf16[64,1152]{1,0:T(8,128)(2,1)S(1)}, bf16[64,1152]{1,0:T(8,128)(2,1)S(1)}, u32[]{:S(2)}, u32[]{:S(2)}) collective-permute-start(bf16[64,1152]{1,0:T(8,128)(2,1)S(1)} %get-tuple-element.39), channel_id=1, source_target_pairs={{0,64},{1,449},{32,96},{33,481},{64,128},{65,1},{96,160},{97,33},{... | collective-permute-start | bytes 442376 | tf_op jit(solution)/shard_map/ppermute | solution.py:185
  67.3 4.1 %collective-permute-done.7.refs_7_ = bf16[64,1152]{1,0:T(8,128)(2,1)S(1)} collective-permute-done((bf16[64,1152]{1,0:T(8,128)(2,1)S(1)}, bf16[64,1152]{1,0:T(8,128)(2,1)S(1)}, u32[]{:S(2)}, u32[]{:S(2)}) %collective-permute-start.7) | collective-permute-done | bytes 147488 | tf_op jit(solution)/shard_map/ppermute | solution.py:185
  71.5 26.5 %all_to_all.20.parts = bf16[4,16,2688]{2,1,0:T(8,128)(2,1)S(1)} all-to-all(bf16[4,16,2688]{2,1,0:T(8,128)(2,1)S(1)} %window.1), channel_id=1, replica_groups=mesh['zh'=4,'zl'=4,'xl'=2,'xh'=2,'y'=4,'core'=2] {'zh'}, dimensions={0} | all-to-all | bytes 688128 | tf_op jit(solution)/shard_map/all_to_all | solution.py:247
  98.0 26.2 %all_to_all.21 = bf16[4,16,2688]{2,1,0:T(8,128)(2,1)S(1)} all-to-all(bf16[4,16,2688]{2,1,0:T(8,128)(2,1)S(1)} %gated.1), channel_id=1, replica_groups=mesh['zh'=4,'zl'=4,'xl'=2,'xh'=2,'y'=4,'core'=2] {'zh'}, dimensions={0} | all-to-all | bytes 688128 | tf_op jit(solution)/shard_map/all_to_all | solution.py:250
  124.2 1.9 %collective-permute-start.10 = (bf16[64,2688]{1,0:T(8,128)(2,1)S(1)}, bf16[64,2688]{1,0:T(8,128)(2,1)S(1)}, u32[]{:S(2)}, u32[]{:S(2)}) collective-permute-start(bf16[64,2688]{1,0:T(8,128)(2,1)S(1)} %bitcast.9), channel_id=1, source_target_pairs={{0,64},{1,449},{32,96},{33,481},{64,128},{65,1},{96,160},{97,33},{... | collective-permute-start | bytes 1032200 | tf_op jit(solution)/shard_map/ppermute | solution.py:185
  126.1 3.9 %collective-permute-start.9 = (bf16[64,2688]{1,0:T(8,128)(2,1)S(1)}, bf16[64,2688]{1,0:T(8,128)(2,1)S(1)}, u32[]{:S(2)}, u32[]{:S(2)}) collective-permute-start(bf16[64,2688]{1,0:T(8,128)(2,1)S(1)} %bitcast.10), channel_id=1, source_target_pairs={{0,480},{1,33},{32,0},{33,65},{64,32},{65,97},{96,64},{97,129},{12... | collective-permute-start | bytes 1032200 | tf_op jit(solution)/shard_map/ppermute | solution.py:185
  130.1 2.5 %collective-permute-start.8 = (bf16[64,2688]{1,0:T(8,128)(2,1)S(1)}, bf16[64,2688]{1,0:T(8,128)(2,1)S(1)}, u32[]{:S(2)}, u32[]{:S(2)}) collective-permute-start(bf16[64,2688]{1,0:T(8,128)(2,1)S(1)} %bitcast.11), channel_id=1, source_target_pairs={{0,32},{1,481},{32,64},{33,1},{64,96},{65,33},{96,128},{97,65},{12... | collective-permute-start | bytes 1032200 | tf_op jit(solution)/shard_map/ppermute | solution.py:185
  132.6 3.4 %collective-permute-done.10.far = bf16[64,2688]{1,0:T(8,128)(2,1)S(1)} collective-permute-done((bf16[64,2688]{1,0:T(8,128)(2,1)S(1)}, bf16[64,2688]{1,0:T(8,128)(2,1)S(1)}, u32[]{:S(2)}, u32[]{:S(2)}) %collective-permute-start.10) | collective-permute-done | bytes 344096 | tf_op jit(solution)/shard_map/ppermute | solution.py:185
  136.0 5.0 %collective-permute-done.9.behind = bf16[64,2688]{1,0:T(8,128)(2,1)S(1)} collective-permute-done((bf16[64,2688]{1,0:T(8,128)(2,1)S(1)}, bf16[64,2688]{1,0:T(8,128)(2,1)S(1)}, u32[]{:S(2)}, u32[]{:S(2)}) %collective-permute-start.9) | collective-permute-done | bytes 344096 | tf_op jit(solution)/shard_map/ppermute | solution.py:185
  141.0 3.1 %collective-permute-done.8.ahead = bf16[64,2688]{1,0:T(8,128)(2,1)S(1)} collective-permute-done((bf16[64,2688]{1,0:T(8,128)(2,1)S(1)}, bf16[64,2688]{1,0:T(8,128)(2,1)S(1)}, u32[]{:S(2)}, u32[]{:S(2)}) %collective-permute-start.8) | collective-permute-done | bytes 344096 | tf_op jit(solution)/shard_map/ppermute | solution.py:185
  145.2 18.1 %all_to_all.22.parts = bf16[32,16,512]{2,1,0:T(8,128)(2,1)S(1)} all-to-all(bf16[32,16,512]{2,1,0:T(8,128)(2,1)S(1)} %bitcast.8), channel_id=1, replica_groups=mesh['zh'=4,'zl'=4,'xl'=2,'xh'=2,'y'=4,'core'=2] {'xl','xh','y','core'}, dimensions={0} | all-to-all | bytes 1048576 | tf_op jit(solution)/shard_map/all_to_all | solution.py:258
  (25 shorter events, 4.6 us)
Async XLA Ops:
  0.6 6.6 %copy-start.3 = (bf16[16,256]{1,0:T(8,128)(2,1)S(1)}, bf16[16,256]{1,0:T(8,128)(2,1)}, u32[]{:S(2)}) copy-start(bf16[16,256]{1,0:T(8,128)(2,1)} %param.9) | copy-start | bytes 24580
  0.6 6.6 %copy-start.4 = (bf16[16,256]{1,0:T(8,128)(2,1)S(1)}, bf16[16,256]{1,0:T(8,128)(2,1)}, u32[]{:S(2)}) copy-start(bf16[16,256]{1,0:T(8,128)(2,1)} %param.8) | copy-start | bytes 24580
  3.2 16.5 %collective-permute-start = (bf16[768,512]{1,0:T(8,128)(2,1)}, bf16[768,512]{1,0:T(8,128)(2,1)S(1)}, u32[]{:S(2)}, u32[]{:S(2)}) collective-permute-start(bf16[768,512]{1,0:T(8,128)(2,1)} %get-tuple-element.24), channel_id=1, source_target_pairs={{0,16},{16,0},{1,17},{17,1},{2,18},{18,2},{3,19},{19,3},{4,20},{20... | collective-permute-start | bytes 2359304 | tf_op jit(solution)/shard_map/ppermute | solution.py:214
  8.1 28.6 %all-to-all-start = ((bf16[32,2,16,256]{3,2,1,0:T(8,128)(2,1)}), bf16[32,2,16,256]{3,2,1,0:T(8,128)(2,1)S(1)}, u32[]{:S(2)}, u32[]{:S(2)}) async-start(bf16[32,2,16,256]{3,2,1,0:T(8,128)(2,1)} %broadcast_in_dim.2), calls=%async_computation | async-start | bytes 1048576 | tf_op jit(solution)/shard_map/all_to_all | solution.py:221
  16.5 3.3 %copy-start.5 = (bf16[768,384]{1,0:T(8,128)(2,1)S(1)}, bf16[768,384]{1,0:T(8,128)(2,1)}, u32[]{:S(2)}) copy-start(bf16[768,384]{1,0:T(8,128)(2,1)} %get-tuple-element.35) | copy-start | bytes 1769476
  19.7 36.3 %collective-permute-start.4 = (bf16[768,384]{1,0:T(8,128)(2,1)S(1)}, bf16[768,384]{1,0:T(8,128)(2,1)S(1)}, u32[]{:S(2)}, u32[]{:S(2)}) collective-permute-start(bf16[768,384]{1,0:T(8,128)(2,1)S(1)} %copy-done.5), channel_id=1, source_target_pairs={{0,16},{16,0},{1,17},{17,1},{2,18},{18,2},{3,19},{19,3},{4,20},{20... | collective-permute-start | bytes 1769480 | tf_op jit(solution)/shard_map/ppermute | solution.py:214
  36.7 1.1 copy-start
  37.8 18.2 %copy-start.2 = (bf16[768,384]{1,0:T(8,128)(2,1)S(1)}, bf16[768,384]{1,0:T(8,128)(2,1)}, u32[]{:S(2)}) copy-start(bf16[768,384]{1,0:T(8,128)(2,1)} %get-tuple-element.34.keep_in.refs_2_) | copy-start | bytes 1769476
  39.1 16.9 %collective-permute-start.1 = (bf16[64,1536]{1,0:T(8,128)(2,1)S(1)}, bf16[64,1536]{1,0:T(8,128)(2,1)S(1)}, u32[]{:S(2)}, u32[]{:S(2)}) collective-permute-start(bf16[64,1536]{1,0:T(8,128)(2,1)S(1)} %get-tuple-element.31), channel_id=1, source_target_pairs={{0,32},{1,481},{32,64},{33,1},{64,96},{65,33},{96,128},{97,65},{12... | collective-permute-start | bytes 589832 | tf_op jit(solution)/shard_map/ppermute | solution.py:185
  50.3 17.0 %collective-permute-start.2 = (bf16[64,1536]{1,0:T(8,128)(2,1)S(1)}, bf16[64,1536]{1,0:T(8,128)(2,1)S(1)}, u32[]{:S(2)}, u32[]{:S(2)}) collective-permute-start(bf16[64,1536]{1,0:T(8,128)(2,1)S(1)} %get-tuple-element.32), channel_id=1, source_target_pairs={{0,480},{1,33},{32,0},{33,65},{64,32},{65,97},{96,64},{97,129},{12... | collective-permute-start | bytes 589832 | tf_op jit(solution)/shard_map/ppermute | solution.py:185
  52.2 15.1 %collective-permute-start.3 = (bf16[64,1536]{1,0:T(8,128)(2,1)S(1)}, bf16[64,1536]{1,0:T(8,128)(2,1)S(1)}, u32[]{:S(2)}, u32[]{:S(2)}) collective-permute-start(bf16[64,1536]{1,0:T(8,128)(2,1)S(1)} %get-tuple-element.33), channel_id=1, source_target_pairs={{0,64},{1,449},{32,96},{33,481},{64,128},{65,1},{96,160},{97,33},{... | collective-permute-start | bytes 589832 | tf_op jit(solution)/shard_map/ppermute | solution.py:185
  57.2 10.1 %collective-permute-start.5 = (bf16[64,1152]{1,0:T(8,128)(2,1)S(1)}, bf16[64,1152]{1,0:T(8,128)(2,1)S(1)}, u32[]{:S(2)}, u32[]{:S(2)}) collective-permute-start(bf16[64,1152]{1,0:T(8,128)(2,1)S(1)} %get-tuple-element.37), channel_id=1, source_target_pairs={{0,32},{1,481},{32,64},{33,1},{64,96},{65,33},{96,128},{97,65},{12... | collective-permute-start | bytes 442376 | tf_op jit(solution)/shard_map/ppermute | solution.py:185
  59.8 7.4 %collective-permute-start.6 = (bf16[64,1152]{1,0:T(8,128)(2,1)S(1)}, bf16[64,1152]{1,0:T(8,128)(2,1)S(1)}, u32[]{:S(2)}, u32[]{:S(2)}) collective-permute-start(bf16[64,1152]{1,0:T(8,128)(2,1)S(1)} %get-tuple-element.38), channel_id=1, source_target_pairs={{0,480},{1,33},{32,0},{33,65},{64,32},{65,97},{96,64},{97,129},{12... | collective-permute-start | bytes 442376 | tf_op jit(solution)/shard_map/ppermute | solution.py:185
  62.9 8.4 %collective-permute-start.7 = (bf16[64,1152]{1,0:T(8,128)(2,1)S(1)}, bf16[64,1152]{1,0:T(8,128)(2,1)S(1)}, u32[]{:S(2)}, u32[]{:S(2)}) collective-permute-start(bf16[64,1152]{1,0:T(8,128)(2,1)S(1)} %get-tuple-element.39), channel_id=1, source_target_pairs={{0,64},{1,449},{32,96},{33,481},{64,128},{65,1},{96,160},{97,33},{... | collective-permute-start | bytes 442376 | tf_op jit(solution)/shard_map/ppermute | solution.py:185
  98.0 46.2 %copy-start.1 = (bf16[768,512]{1,0:T(8,128)(2,1)S(1)}, bf16[768,512]{1,0:T(8,128)(2,1)}, u32[]{:S(2)}) copy-start(bf16[768,512]{1,0:T(8,128)(2,1)} %get-tuple-element.28.keep_in.refs_0_) | copy-start | bytes 2359300
  124.2 11.8 %collective-permute-start.10 = (bf16[64,2688]{1,0:T(8,128)(2,1)S(1)}, bf16[64,2688]{1,0:T(8,128)(2,1)S(1)}, u32[]{:S(2)}, u32[]{:S(2)}) collective-permute-start(bf16[64,2688]{1,0:T(8,128)(2,1)S(1)} %bitcast.9), channel_id=1, source_target_pairs={{0,64},{1,449},{32,96},{33,481},{64,128},{65,1},{96,160},{97,33},{... | collective-permute-start | bytes 1032200 | tf_op jit(solution)/shard_map/ppermute | solution.py:185
  126.1 14.9 %collective-permute-start.9 = (bf16[64,2688]{1,0:T(8,128)(2,1)S(1)}, bf16[64,2688]{1,0:T(8,128)(2,1)S(1)}, u32[]{:S(2)}, u32[]{:S(2)}) collective-permute-start(bf16[64,2688]{1,0:T(8,128)(2,1)S(1)} %bitcast.10), channel_id=1, source_target_pairs={{0,480},{1,33},{32,0},{33,65},{64,32},{65,97},{96,64},{97,129},{12... | collective-permute-start | bytes 1032200 | tf_op jit(solution)/shard_map/ppermute | solution.py:185
  130.1 14.1 %collective-permute-start.8 = (bf16[64,2688]{1,0:T(8,128)(2,1)S(1)}, bf16[64,2688]{1,0:T(8,128)(2,1)S(1)}, u32[]{:S(2)}, u32[]{:S(2)}) collective-permute-start(bf16[64,2688]{1,0:T(8,128)(2,1)S(1)} %bitcast.11), channel_id=1, source_target_pairs={{0,32},{1,481},{32,64},{33,1},{64,96},{65,33},{96,128},{97,65},{12... | collective-permute-start | bytes 1032200 | tf_op jit(solution)/shard_map/ppermute | solution.py:185

commit v3 on v2

--- a/solution.py
+++ b/solution.py
@@ -107,18 +107,19 @@
 
 
 def window_kernel(*refs):
-    out, left = refs[-1], 0
-    n = out.shape[1]
-    for k in range(0, len(refs) - 1, 4):
+    here, ahead, far, behind, buf = refs[-5:]
+    zh, turn = lax.axis_index("zh"), toward()
+    n, left = here.shape[0], 0
+    for k in range(0, len(refs) - 5, 4):
         own, *parts = refs[k : k + 4]
-        width = own.shape[1]
-        for i in range(out.shape[0]):
-            rows = slice(i * n, (i + 1) * n)
-            total = own[rows, :]
-            for part in parts:
-                total = total + part[rows, :].astype(F32)
-            out[i, :, left : left + width] = total.astype(BF16)
-        left += width
+        total = own[...]
+        for part in parts:
+            total = total + part[...].astype(F32)
+        buf[:, left : left + own.shape[1]] = total
+        left += own.shape[1]
+    for shift, out in ((2, far), (-turn, behind), (turn, ahead), (0, here)):
+        at = pl.ds(pl.multiple_of(lax.rem(zh + shift + 4, 4) * n, n), n)
+        out[...] = buf[at, :].astype(out.dtype)
 
 
 def spans(widths):
@@ -129,12 +130,9 @@
     return at
 
 
-def gated_kernel(widths, parts, out):
+def gated_kernel(widths, here, direct, passed, out):
     def total(cols):
-        s = parts[0, :, cols].astype(F32)
-        for i in range(1, parts.shape[0]):
-            s = s + parts[i, :, cols].astype(F32)
-        return s
+        return here[:, cols] + direct[:, cols].astype(F32) + passed[:, cols].astype(F32)
 
     for at in spans(widths):
         gate_sum, up_sum, back_sum = (total(cols) for cols in at)
@@ -146,19 +144,20 @@
             back_sum * active,
         )
         for cols, result in zip(at, results):
-            for i in range(out.shape[0]):
-                out[i, :, cols] = result.astype(BF16)
+            out[:, cols] = result.astype(BF16)
 
 
 def output_kernel(widths, own, ahead, behind, far, *refs):
     weights, out, rows = refs[:-2], refs[-2], refs[-1]
-    xl, zl, turn = lax.axis_index("xl"), lax.axis_index("zl"), toward()
+    xl, turn = lax.axis_index("xl"), toward()
+    z = lax.axis_index("zh") * 4 + lax.axis_index("zl")
     n = out.shape[1] // 16
     depth = weights[0].shape[0] // 3
-    for shift, src in ((0, own), (-turn, ahead), (turn, behind), (2, far)):
-        cls = lax.rem(zl + shift + 4, 4)
-        for i in range(4):
-            at = pl.ds(pl.multiple_of((i * 4 + cls) * n, n), n)
+    for shift, src in ((0, own), (-turn, ahead), (turn, behind), (-2 * turn, far)):
+        sender = lax.rem(z + shift + 16, 16)
+        for i, step in enumerate((0, -turn, 2, turn)):
+            block = lax.rem(lax.div(sender, 4) + step + 4, 4) * 4 + lax.rem(sender, 4)
+            at = pl.ds(pl.multiple_of(block * n, n), n)
             rows[at, :] = src[i * n : (i + 1) * n, :]
     for k, x in enumerate((xl, 1 - xl)):
         mixed = grad = 0.0
@@ -240,14 +239,21 @@
         )
         windows += [own, *exchange(parts)]
         weights += [keep, other]
-    (window,) = call(window_kernel, [((4, n_tok, w), BF16)], windows, "window")
-    (spread,) = call(
-        functools.partial(gated_kernel, widths),
-        [((4, n_tok, w), BF16)],
-        (lax.all_to_all(window, "zh", 0, 0, tiled=True),),
-        "gated",
-    )
-    mine = lax.all_to_all(spread, "zh", 0, 0, tiled=True).reshape(n, w)
+    here, ahead, far, behind = call(
+        window_kernel,
+        [((n_tok, w), F32)] * 2 + [((n_tok, w), BF16)] * 2,
+        windows,
+        "window",
+        scratch=[pltpu.VMEM((n, w), F32)],
+    )
+    passed = along_z(far, 4)
+    direct = along_z(behind, -4)
+    passed = along_z((ahead + passed.astype(F32)).astype(BF16), 4)
+    (mine,) = call(
+        functools.partial(gated_kernel, widths), [((n_tok, w), BF16)], (here, direct, passed), "gated"
+    )
+    one, three = along_z(mine, 4), along_z(mine, -4)
+    mine = jnp.concatenate([mine, one, along_z(one, 4), three])
     (shares,) = call(
         functools.partial(output_kernel, widths),
         [((2, 16 * n_tok, 2 * depth), BF16)],

time: 165 us -> 161 us (0.976)
  blocking collectives: 70.7 us -> 25.4 us
  starting transfers between devices: 51.6 us -> 78.8 us
  waiting for transfers between devices: 29.2 us -> 43.4 us
    all_to_all x2 -> x0, blocking collectives: 52.6 us -> none  [the longest x1 26.5 us: shards(): lax.all_to_all(window, 'zh', 0, 0, tiled=True)]
    ppermute x9 -> x15, starting transfers between devices: 35.3 us -> 62.4 us  [along_z(): return lax.ppermute(x, Z + ('core',), pairs)]
    ppermute x9 -> x15, waiting for transfers between devices: 15.6 us -> 29.8 us  [along_z(): return lax.ppermute(x, Z + ('core',), pairs)]
    all_to_all x1, blocking collectives: 18.1 us -> 25.4 us  [shards(): lax.all_to_all(shares.reshape(32, n_tok, 2 * depth), ('xl',) + TP, 0, 0,...]
  transfers between devices with their start and end apart: 12 -> 18, of which waited for: 6 -> 10; matrix products, arithmetic and copies ran while one was open for 1% -> 1% of each run, Pallas kernels for 3% -> 3%
where the time goes in v3:
time: 161 us; the launch traced here: 160 us
  starting transfers between devices  78.8 us (49%)
  waiting for transfers between devices  43.4 us (27%)
  blocking collectives  25.4 us (16%)
  Pallas kernels  9.63 us (6%)
  local copies, waits for them, and re-layouts  2.01 us (1%)
    ppermute x15, starting transfers between devices, along_z(): return lax.ppermute(x, Z + ('core',), pairs)  62.4 us
    ppermute x15, waiting for transfers between devices, along_z(): return lax.ppermute(x, Z + ('core',), pairs)  29.8 us
    all_to_all x1, blocking collectives, shards(): lax.all_to_all(shares.reshape(32, n_tok, 2 * depth), ('xl',) + TP, 0, 0,...  25.4 us
    all_to_all x1, waiting for transfers between devices, shards(): lax.all_to_all(jnp.broadcast_to(acts[None], (32,) + acts.shape), ('xl',)...  12.9 us
    pallas_call x8, Pallas kernels, call(): pl.pallas_call(body, out_shape=[jax.ShapeDtypeStruct(s, d) for s, d in ou...  9.63 us
    all_to_all x1, starting transfers between devices, shards(): lax.all_to_all(jnp.broadcast_to(acts[None], (32,) + acts.shape), ('xl',)...  8.39 us
    ppermute x2, starting transfers between devices, swap(): return lax.ppermute(x, 'xl', [(0, 1), (1, 0)])  7.94 us
  transfers between devices with their start and end apart: 18, of which 10 were waited for; matrix products, arithmetic and copies ran while one was open for 1% of the time, Pallas kernels for 3%

profile of v3, /device:TPU:1, one launch (start us, length us, event | category | flops | bytes accessed | tf_op | source)
XLA Modules:
  0.0 160.2 jit_solution(15257402633736995469)
XLA Ops:
  0.6 2.6 %scaled.2 = (bf16[768,512]{1,0:T(8,128)(2,1)}, bf16[768,384]{1,0:T(8,128)(2,1)}) custom-call(f32[2,14]{1,0:T(2,128)} %refs_0_.3, f32[2,14]{1,0:T(2,128)} %refs_1_.3, f32[2,14]{1,0:T(2,128)} %bitcast.10, bf16[256,1792]{1,0:T(8,128)(2,1)} %refs_3_.3, bf16[256,1792]{1,0:T(8,128)(2,1)} %refs_4_.3, bf16[1792,256]{1,0:T(8,128)(2,1)} %refs_5_.3), custom_call_target="tpu_custom_call" | custom-call | tf_op jit(solution)/shard_map/scaled/pallas_call | solution.py:21
  3.2 3.9 %collective-permute-start = (bf16[768,512]{1,0:T(8,128)(2,1)}, bf16[768,512]{1,0:T(8,128)(2,1)S(1)}, u32[]{:S(2)}, u32[]{:S(2)}) collective-permute-start(bf16[768,512]{1,0:T(8,128)(2,1)} %get-tuple-element.28), channel_id=1, source_target_pairs={{0,16},{16,0},{1,17},{17,1},{2,18},{18,2},{3,19},{19,3},{4,20},{20... | collective-permute-start | bytes 2359304 | tf_op jit(solution)/shard_map/ppermute | solution.py:213
  8.1 8.4 %all-to-all-start = ((bf16[32,2,16,256]{3,2,1,0:T(8,128)(2,1)}), bf16[32,2,16,256]{3,2,1,0:T(8,128)(2,1)S(1)}, u32[]{:S(2)}, u32[]{:S(2)}) async-start(bf16[32,2,16,256]{3,2,1,0:T(8,128)(2,1)} %broadcast_in_dim.2), calls=%async_computation | async-start | bytes 1048576 | tf_op jit(solution)/shard_map/all_to_all | solution.py:220
  16.5 2.6 %scaled.3 = (bf16[768,512]{1,0:T(8,128)(2,1)}, bf16[768,384]{1,0:T(8,128)(2,1)}) custom-call(f32[2,14]{1,0:T(2,128)} %refs_0_.3, f32[2,14]{1,0:T(2,128)} %refs_1_.3, f32[2,14]{1,0:T(2,128)} %bitcast.11, bf16[256,1792]{1,0:T(8,128)(2,1)} %refs_3_.3, bf16[256,1792]{1,0:T(8,128)(2,1)} %refs_4_.3, bf16[1792,256]{1,0:T(8,128)(2,1)} %refs_5_.3), custom_call_target="tpu_custom_call" | custom-call | tf_op jit(solution)/shard_map/scaled/pallas_call | solution.py:21
  19.7 4.0 %collective-permute-start.4 = (bf16[768,384]{1,0:T(8,128)(2,1)S(1)}, bf16[768,384]{1,0:T(8,128)(2,1)S(1)}, u32[]{:S(2)}, u32[]{:S(2)}) collective-permute-start(bf16[768,384]{1,0:T(8,128)(2,1)S(1)} %copy-done.5), channel_id=1, source_target_pairs={{0,16},{16,0},{1,17},{17,1},{2,18},{18,2},{3,19},{19,3},{4,20},{20... | collective-permute-start | bytes 1769480 | tf_op jit(solution)/shard_map/ppermute | solution.py:213
  23.7 12.9 %all-to-all-done = bf16[32,2,16,256]{3,2,1,0:T(8,128)(2,1)S(1)} async-done(((bf16[32,2,16,256]{3,2,1,0:T(8,128)(2,1)}), bf16[32,2,16,256]{3,2,1,0:T(8,128)(2,1)S(1)}, u32[]{:S(2)}, u32[]{:S(2)}) %all-to-all-start) | async-done | bytes 524320 | tf_op jit(solution)/shard_map/all_to_all | solution.py:220
  39.1 11.1 %collective-permute-start.1 = (bf16[64,1536]{1,0:T(8,128)(2,1)S(1)}, bf16[64,1536]{1,0:T(8,128)(2,1)S(1)}, u32[]{:S(2)}, u32[]{:S(2)}) collective-permute-start(bf16[64,1536]{1,0:T(8,128)(2,1)S(1)} %get-tuple-element.35), channel_id=1, source_target_pairs={{0,32},{1,481},{32,64},{33,1},{64,96},{65,33},{96,128},{97,65},{12... | collective-permute-start | bytes 589832 | tf_op jit(solution)/shard_map/ppermute | solution.py:184
  52.2 3.8 %collective-permute-start.3 = (bf16[64,1536]{1,0:T(8,128)(2,1)S(1)}, bf16[64,1536]{1,0:T(8,128)(2,1)S(1)}, u32[]{:S(2)}, u32[]{:S(2)}) collective-permute-start(bf16[64,1536]{1,0:T(8,128)(2,1)S(1)} %get-tuple-element.37), channel_id=1, source_target_pairs={{0,64},{1,449},{32,96},{33,481},{64,128},{65,1},{96,160},{97,33},{... | collective-permute-start | bytes 589832 | tf_op jit(solution)/shard_map/ppermute | solution.py:184
  57.2 2.7 %collective-permute-start.5 = (bf16[64,1152]{1,0:T(8,128)(2,1)S(1)}, bf16[64,1152]{1,0:T(8,128)(2,1)S(1)}, u32[]{:S(2)}, u32[]{:S(2)}) collective-permute-start(bf16[64,1152]{1,0:T(8,128)(2,1)S(1)} %get-tuple-element.41), channel_id=1, source_target_pairs={{0,32},{1,481},{32,64},{33,1},{64,96},{65,33},{96,128},{97,65},{12... | collective-permute-start | bytes 442376 | tf_op jit(solution)/shard_map/ppermute | solution.py:184
  59.8 3.1 %collective-permute-start.6 = (bf16[64,1152]{1,0:T(8,128)(2,1)S(1)}, bf16[64,1152]{1,0:T(8,128)(2,1)S(1)}, u32[]{:S(2)}, u32[]{:S(2)}) collective-permute-start(bf16[64,1152]{1,0:T(8,128)(2,1)S(1)} %get-tuple-element.42), channel_id=1, source_target_pairs={{0,480},{1,33},{32,0},{33,65},{64,32},{65,97},{96,64},{97,129},{12... | collective-permute-start | bytes 442376 | tf_op jit(solution)/shard_map/ppermute | solution.py:184
  62.9 4.3 %collective-permute-start.7 = (bf16[64,1152]{1,0:T(8,128)(2,1)S(1)}, bf16[64,1152]{1,0:T(8,128)(2,1)S(1)}, u32[]{:S(2)}, u32[]{:S(2)}) collective-permute-start(bf16[64,1152]{1,0:T(8,128)(2,1)S(1)} %get-tuple-element.43), channel_id=1, source_target_pairs={{0,64},{1,449},{32,96},{33,481},{64,128},{65,1},{96,160},{97,33},{... | collective-permute-start | bytes 442376 | tf_op jit(solution)/shard_map/ppermute | solution.py:184
  67.3 4.1 %collective-permute-done.7.refs_7_ = bf16[64,1152]{1,0:T(8,128)(2,1)S(1)} collective-permute-done((bf16[64,1152]{1,0:T(8,128)(2,1)S(1)}, bf16[64,1152]{1,0:T(8,128)(2,1)S(1)}, u32[]{:S(2)}, u32[]{:S(2)}) %collective-permute-start.7) | collective-permute-done | bytes 147488 | tf_op jit(solution)/shard_map/ppermute | solution.py:184
  71.6 5.0 %collective-permute-start.9 = (bf16[16,2688]{1,0:T(8,128)(2,1)S(1)}, bf16[16,2688]{1,0:T(8,128)(2,1)S(1)}, u32[]{:S(2)}, u32[]{:S(2)}) collective-permute-start(bf16[16,2688]{1,0:T(8,128)(2,1)S(1)} %get-tuple-element.47), channel_id=1, source_target_pairs={{0,128},{1,385},{32,160},{33,417},{64,192},{65,449},{96,224},{97,4... | collective-permute-start | bytes 258056 | tf_op jit(solution)/shard_map/ppermute | solution.py:184
  76.6 4.3 %collective-permute-start.8 = (bf16[16,2688]{1,0:T(8,128)(2,1)S(1)}, bf16[16,2688]{1,0:T(8,128)(2,1)S(1)}, u32[]{:S(2)}, u32[]{:S(2)}) collective-permute-start(bf16[16,2688]{1,0:T(8,128)(2,1)S(1)} %get-tuple-element.45), channel_id=1, source_target_pairs={{0,384},{1,129},{32,416},{33,161},{64,448},{65,193},{96,480},{97,2... | collective-permute-start | bytes 258056 | tf_op jit(solution)/shard_map/ppermute | solution.py:184
  82.7 3.2 %collective-permute-start.10 = (bf16[16,2688]{1,0:T(8,128)(2,1)S(1)}, bf16[16,2688]{1,0:T(8,128)(2,1)S(1)}, u32[]{:S(2)}, u32[]{:S(2)}) collective-permute-start(bf16[16,2688]{1,0:T(8,128)(2,1)S(1)} %add_convert_fusion), channel_id=1, source_target_pairs={{0,128},{1,385},{32,160},{33,417},{64,192},{65,449},{96,224},{97,4... | collective-permute-start | bytes 258056 | tf_op jit(solution)/shard_map/ppermute | solution.py:184
  85.9 2.4 %collective-permute-done.8.direct = bf16[16,2688]{1,0:T(8,128)(2,1)S(1)} collective-permute-done((bf16[16,2688]{1,0:T(8,128)(2,1)S(1)}, bf16[16,2688]{1,0:T(8,128)(2,1)S(1)}, u32[]{:S(2)}, u32[]{:S(2)}) %collective-permute-start.8) | collective-permute-done | bytes 86048 | tf_op jit(solution)/shard_map/ppermute | solution.py:184
  88.3 5.9 %collective-permute-done.10.passed = bf16[16,2688]{1,0:T(8,128)(2,1)S(1)} collective-permute-done((bf16[16,2688]{1,0:T(8,128)(2,1)S(1)}, bf16[16,2688]{1,0:T(8,128)(2,1)S(1)}, u32[]{:S(2)}, u32[]{:S(2)}) %collective-permute-start.10) | collective-permute-done | bytes 86048 | tf_op jit(solution)/shard_map/ppermute | solution.py:184
  96.1 7.3 %collective-permute-start.13 = (bf16[16,2688]{1,0:T(8,128)(2,1)S(1)}, bf16[16,2688]{1,0:T(8,128)(2,1)S(1)}, u32[]{:S(2)}, u32[]{:S(2)}) collective-permute-start(bf16[16,2688]{1,0:T(8,128)(2,1)S(1)} %gated.1), channel_id=1, source_target_pairs={{0,384},{1,129},{32,416},{33,161},{64,448},{65,193},{96,480},{97,2... | collective-permute-start | bytes 258056 | tf_op jit(solution)/shard_map/ppermute | solution.py:184
  103.5 2.8 %collective-permute-start.12 = (bf16[16,2688]{1,0:T(8,128)(2,1)S(1)}, bf16[16,2688]{1,0:T(8,128)(2,1)S(1)}, u32[]{:S(2)}, u32[]{:S(2)}) collective-permute-start(bf16[16,2688]{1,0:T(8,128)(2,1)S(1)} %collective-permute-done.11), channel_id=1, source_target_pairs={{0,128},{1,385},{32,160},{33,417},{64,192},{65,449},{96,224},{97,4... | collective-permute-start | bytes 258056 | tf_op jit(solution)/shard_map/ppermute | solution.py:184
  106.7 7.3 %collective-permute-done.12 = bf16[16,2688]{1,0:T(8,128)(2,1)S(1)} collective-permute-done((bf16[16,2688]{1,0:T(8,128)(2,1)S(1)}, bf16[16,2688]{1,0:T(8,128)(2,1)S(1)}, u32[]{:S(2)}, u32[]{:S(2)}) %collective-permute-start.12) | collective-permute-done | bytes 86048 | tf_op jit(solution)/shard_map/ppermute | solution.py:184
  114.1 2.0 %collective-permute-start.16 = (bf16[64,2688]{1,0:T(8,128)(2,1)S(1)}, bf16[64,2688]{1,0:T(8,128)(2,1)S(1)}, u32[]{:S(2)}, u32[]{:S(2)}) collective-permute-start(bf16[64,2688]{1,0:T(8,128)(2,1)S(1)} %pad_maximum_fusion.own), channel_id=1, source_target_pairs={{0,64},{1,449},{32,96},{33,481},{64,128},{65,1},{96,160},{97,33},{... | collective-permute-start | bytes 1032200 | tf_op jit(solution)/shard_map/ppermute | solution.py:184
  116.1 7.1 %collective-permute-start.15 = (bf16[64,2688]{1,0:T(8,128)(2,1)S(1)}, bf16[64,2688]{1,0:T(8,128)(2,1)S(1)}, u32[]{:S(2)}, u32[]{:S(2)}) collective-permute-start(bf16[64,2688]{1,0:T(8,128)(2,1)S(1)} %pad_maximum_fusion.own), channel_id=1, source_target_pairs={{0,480},{1,33},{32,0},{33,65},{64,32},{65,97},{96,64},{97,129},{12... | collective-permute-start | bytes 1032200 | tf_op jit(solution)/shard_map/ppermute | solution.py:184
  125.1 7.1 %collective-permute-done.15.behind = bf16[64,2688]{1,0:T(8,128)(2,1)S(1)} collective-permute-done((bf16[64,2688]{1,0:T(8,128)(2,1)S(1)}, bf16[64,2688]{1,0:T(8,128)(2,1)S(1)}, u32[]{:S(2)}, u32[]{:S(2)}) %collective-permute-start.15) | collective-permute-done | bytes 344096 | tf_op jit(solution)/shard_map/ppermute | solution.py:184
  134.2 25.4 %all_to_all.10.parts = bf16[32,16,512]{2,1,0:T(8,128)(2,1)S(1)} all-to-all(bf16[32,16,512]{2,1,0:T(8,128)(2,1)S(1)} %bitcast.7), channel_id=1, replica_groups=mesh['zh'=4,'zl'=4,'xl'=2,'xh'=2,'y'=4,'core'=2] {'xl','xh','y','core'}, dimensions={0} | all-to-all | bytes 1048576 | tf_op jit(solution)/shard_map/all_to_all | solution.py:264
  (37 shorter events, 16.1 us)
Async XLA Ops:
  0.6 6.6 %copy-start.3 = (bf16[16,256]{1,0:T(8,128)(2,1)S(1)}, bf16[16,256]{1,0:T(8,128)(2,1)}, u32[]{:S(2)}) copy-start(bf16[16,256]{1,0:T(8,128)(2,1)} %param.9) | copy-start | bytes 24580
  0.6 6.6 %copy-start.4 = (bf16[16,256]{1,0:T(8,128)(2,1)S(1)}, bf16[16,256]{1,0:T(8,128)(2,1)}, u32[]{:S(2)}) copy-start(bf16[16,256]{1,0:T(8,128)(2,1)} %param.8) | copy-start | bytes 24580
  3.2 16.5 %collective-permute-start = (bf16[768,512]{1,0:T(8,128)(2,1)}, bf16[768,512]{1,0:T(8,128)(2,1)S(1)}, u32[]{:S(2)}, u32[]{:S(2)}) collective-permute-start(bf16[768,512]{1,0:T(8,128)(2,1)} %get-tuple-element.28), channel_id=1, source_target_pairs={{0,16},{16,0},{1,17},{17,1},{2,18},{18,2},{3,19},{19,3},{4,20},{20... | collective-permute-start | bytes 2359304 | tf_op jit(solution)/shard_map/ppermute | solution.py:213
  8.1 28.6 %all-to-all-start = ((bf16[32,2,16,256]{3,2,1,0:T(8,128)(2,1)}), bf16[32,2,16,256]{3,2,1,0:T(8,128)(2,1)S(1)}, u32[]{:S(2)}, u32[]{:S(2)}) async-start(bf16[32,2,16,256]{3,2,1,0:T(8,128)(2,1)} %broadcast_in_dim.2), calls=%async_computation | async-start | bytes 1048576 | tf_op jit(solution)/shard_map/all_to_all | solution.py:220
  16.5 3.3 %copy-start.5 = (bf16[768,384]{1,0:T(8,128)(2,1)S(1)}, bf16[768,384]{1,0:T(8,128)(2,1)}, u32[]{:S(2)}) copy-start(bf16[768,384]{1,0:T(8,128)(2,1)} %get-tuple-element.39) | copy-start | bytes 1769476
  19.7 36.3 %collective-permute-start.4 = (bf16[768,384]{1,0:T(8,128)(2,1)S(1)}, bf16[768,384]{1,0:T(8,128)(2,1)S(1)}, u32[]{:S(2)}, u32[]{:S(2)}) collective-permute-start(bf16[768,384]{1,0:T(8,128)(2,1)S(1)} %copy-done.5), channel_id=1, source_target_pairs={{0,16},{16,0},{1,17},{17,1},{2,18},{18,2},{3,19},{19,3},{4,20},{20... | collective-permute-start | bytes 1769480 | tf_op jit(solution)/shard_map/ppermute | solution.py:213
  36.7 1.1 copy-start
  37.8 18.2 %copy-start.2 = (bf16[768,384]{1,0:T(8,128)(2,1)S(1)}, bf16[768,384]{1,0:T(8,128)(2,1)}, u32[]{:S(2)}) copy-start(bf16[768,384]{1,0:T(8,128)(2,1)} %get-tuple-element.38.keep_in.refs_2_) | copy-start | bytes 1769476
  39.1 16.9 %collective-permute-start.1 = (bf16[64,1536]{1,0:T(8,128)(2,1)S(1)}, bf16[64,1536]{1,0:T(8,128)(2,1)S(1)}, u32[]{:S(2)}, u32[]{:S(2)}) collective-permute-start(bf16[64,1536]{1,0:T(8,128)(2,1)S(1)} %get-tuple-element.35), channel_id=1, source_target_pairs={{0,32},{1,481},{32,64},{33,1},{64,96},{65,33},{96,128},{97,65},{12... | collective-permute-start | bytes 589832 | tf_op jit(solution)/shard_map/ppermute | solution.py:184
  50.3 17.0 %collective-permute-start.2 = (bf16[64,1536]{1,0:T(8,128)(2,1)S(1)}, bf16[64,1536]{1,0:T(8,128)(2,1)S(1)}, u32[]{:S(2)}, u32[]{:S(2)}) collective-permute-start(bf16[64,1536]{1,0:T(8,128)(2,1)S(1)} %get-tuple-element.36), channel_id=1, source_target_pairs={{0,480},{1,33},{32,0},{33,65},{64,32},{65,97},{96,64},{97,129},{12... | collective-permute-start | bytes 589832 | tf_op jit(solution)/shard_map/ppermute | solution.py:184
  52.2 15.1 %collective-permute-start.3 = (bf16[64,1536]{1,0:T(8,128)(2,1)S(1)}, bf16[64,1536]{1,0:T(8,128)(2,1)S(1)}, u32[]{:S(2)}, u32[]{:S(2)}) collective-permute-start(bf16[64,1536]{1,0:T(8,128)(2,1)S(1)} %get-tuple-element.37), channel_id=1, source_target_pairs={{0,64},{1,449},{32,96},{33,481},{64,128},{65,1},{96,160},{97,33},{... | collective-permute-start | bytes 589832 | tf_op jit(solution)/shard_map/ppermute | solution.py:184
  57.2 10.1 %collective-permute-start.5 = (bf16[64,1152]{1,0:T(8,128)(2,1)S(1)}, bf16[64,1152]{1,0:T(8,128)(2,1)S(1)}, u32[]{:S(2)}, u32[]{:S(2)}) collective-permute-start(bf16[64,1152]{1,0:T(8,128)(2,1)S(1)} %get-tuple-element.41), channel_id=1, source_target_pairs={{0,32},{1,481},{32,64},{33,1},{64,96},{65,33},{96,128},{97,65},{12... | collective-permute-start | bytes 442376 | tf_op jit(solution)/shard_map/ppermute | solution.py:184
  59.8 7.4 %collective-permute-start.6 = (bf16[64,1152]{1,0:T(8,128)(2,1)S(1)}, bf16[64,1152]{1,0:T(8,128)(2,1)S(1)}, u32[]{:S(2)}, u32[]{:S(2)}) collective-permute-start(bf16[64,1152]{1,0:T(8,128)(2,1)S(1)} %get-tuple-element.42), channel_id=1, source_target_pairs={{0,480},{1,33},{32,0},{33,65},{64,32},{65,97},{96,64},{97,129},{12... | collective-permute-start | bytes 442376 | tf_op jit(solution)/shard_map/ppermute | solution.py:184
  62.9 8.4 %collective-permute-start.7 = (bf16[64,1152]{1,0:T(8,128)(2,1)S(1)}, bf16[64,1152]{1,0:T(8,128)(2,1)S(1)}, u32[]{:S(2)}, u32[]{:S(2)}) collective-permute-start(bf16[64,1152]{1,0:T(8,128)(2,1)S(1)} %get-tuple-element.43), channel_id=1, source_target_pairs={{0,64},{1,449},{32,96},{33,481},{64,128},{65,1},{96,160},{97,33},{... | collective-permute-start | bytes 442376 | tf_op jit(solution)/shard_map/ppermute | solution.py:184
  71.6 61.5 %copy-start.1 = (bf16[768,512]{1,0:T(8,128)(2,1)S(1)}, bf16[768,512]{1,0:T(8,128)(2,1)}, u32[]{:S(2)}) copy-start(bf16[768,512]{1,0:T(8,128)(2,1)} %get-tuple-element.32.keep_in.refs_0_) | copy-start | bytes 2359300
  71.6 11.1 %collective-permute-start.9 = (bf16[16,2688]{1,0:T(8,128)(2,1)S(1)}, bf16[16,2688]{1,0:T(8,128)(2,1)S(1)}, u32[]{:S(2)}, u32[]{:S(2)}) collective-permute-start(bf16[16,2688]{1,0:T(8,128)(2,1)S(1)} %get-tuple-element.47), channel_id=1, source_target_pairs={{0,128},{1,385},{32,160},{33,417},{64,192},{65,449},{96,224},{97,4... | collective-permute-start | bytes 258056 | tf_op jit(solution)/shard_map/ppermute | solution.py:184
  76.6 11.6 %collective-permute-start.8 = (bf16[16,2688]{1,0:T(8,128)(2,1)S(1)}, bf16[16,2688]{1,0:T(8,128)(2,1)S(1)}, u32[]{:S(2)}, u32[]{:S(2)}) collective-permute-start(bf16[16,2688]{1,0:T(8,128)(2,1)S(1)} %get-tuple-element.45), channel_id=1, source_target_pairs={{0,384},{1,129},{32,416},{33,161},{64,448},{65,193},{96,480},{97,2... | collective-permute-start | bytes 258056 | tf_op jit(solution)/shard_map/ppermute | solution.py:184
  82.7 11.4 %collective-permute-start.10 = (bf16[16,2688]{1,0:T(8,128)(2,1)S(1)}, bf16[16,2688]{1,0:T(8,128)(2,1)S(1)}, u32[]{:S(2)}, u32[]{:S(2)}) collective-permute-start(bf16[16,2688]{1,0:T(8,128)(2,1)S(1)} %add_convert_fusion), channel_id=1, source_target_pairs={{0,128},{1,385},{32,160},{33,417},{64,192},{65,449},{96,224},{97,4... | collective-permute-start | bytes 258056 | tf_op jit(solution)/shard_map/ppermute | solution.py:184
  94.2 9.3 %collective-permute-start.11 = (bf16[16,2688]{1,0:T(8,128)(2,1)S(1)}, bf16[16,2688]{1,0:T(8,128)(2,1)S(1)}, u32[]{:S(2)}, u32[]{:S(2)}) collective-permute-start(bf16[16,2688]{1,0:T(8,128)(2,1)S(1)} %gated.1), channel_id=1, source_target_pairs={{0,128},{1,385},{32,160},{33,417},{64,192},{65,449},{96,224},{97,4... | collective-permute-start | bytes 258056 | tf_op jit(solution)/shard_map/ppermute | solution.py:184
  96.1 10.6 %collective-permute-start.13 = (bf16[16,2688]{1,0:T(8,128)(2,1)S(1)}, bf16[16,2688]{1,0:T(8,128)(2,1)S(1)}, u32[]{:S(2)}, u32[]{:S(2)}) collective-permute-start(bf16[16,2688]{1,0:T(8,128)(2,1)S(1)} %gated.1), channel_id=1, source_target_pairs={{0,384},{1,129},{32,416},{33,161},{64,448},{65,193},{96,480},{97,2... | collective-permute-start | bytes 258056 | tf_op jit(solution)/shard_map/ppermute | solution.py:184
  103.5 10.5 %collective-permute-start.12 = (bf16[16,2688]{1,0:T(8,128)(2,1)S(1)}, bf16[16,2688]{1,0:T(8,128)(2,1)S(1)}, u32[]{:S(2)}, u32[]{:S(2)}) collective-permute-start(bf16[16,2688]{1,0:T(8,128)(2,1)S(1)} %collective-permute-done.11), channel_id=1, source_target_pairs={{0,128},{1,385},{32,160},{33,417},{64,192},{65,449},{96,224},{97,4... | collective-permute-start | bytes 258056 | tf_op jit(solution)/shard_map/ppermute | solution.py:184
  114.1 11.1 %collective-permute-start.16 = (bf16[64,2688]{1,0:T(8,128)(2,1)S(1)}, bf16[64,2688]{1,0:T(8,128)(2,1)S(1)}, u32[]{:S(2)}, u32[]{:S(2)}) collective-permute-start(bf16[64,2688]{1,0:T(8,128)(2,1)S(1)} %pad_maximum_fusion.own), channel_id=1, source_target_pairs={{0,64},{1,449},{32,96},{33,481},{64,128},{65,1},{96,160},{97,33},{... | collective-permute-start | bytes 1032200 | tf_op jit(solution)/shard_map/ppermute | solution.py:184
  116.1 16.1 %collective-permute-start.15 = (bf16[64,2688]{1,0:T(8,128)(2,1)S(1)}, bf16[64,2688]{1,0:T(8,128)(2,1)S(1)}, u32[]{:S(2)}, u32[]{:S(2)}) collective-permute-start(bf16[64,2688]{1,0:T(8,128)(2,1)S(1)} %pad_maximum_fusion.own), channel_id=1, source_target_pairs={{0,480},{1,33},{32,0},{33,65},{64,32},{65,97},{96,64},{97,129},{12... | collective-permute-start | bytes 1032200 | tf_op jit(solution)/shard_map/ppermute | solution.py:184
  123.2 9.9 %collective-permute-start.14 = (bf16[64,2688]{1,0:T(8,128)(2,1)S(1)}, bf16[64,2688]{1,0:T(8,128)(2,1)S(1)}, u32[]{:S(2)}, u32[]{:S(2)}) collective-permute-start(bf16[64,2688]{1,0:T(8,128)(2,1)S(1)} %pad_maximum_fusion.own), channel_id=1, source_target_pairs={{0,32},{1,481},{32,64},{33,1},{64,96},{65,33},{96,128},{97,65},{12... | collective-permute-start | bytes 1032200 | tf_op jit(solution)/shard_map/ppermute | solution.py:184

commit v4 on v3

--- a/solution.py
+++ b/solution.py
@@ -220,14 +220,14 @@
     acts = lax.all_to_all(
         jnp.broadcast_to(acts[None], (32,) + acts.shape), ("xl",) + TP, 0, 0, tiled=True
     ).reshape(2, 16, 2, n_tok, depth)
-    first_other, second, keeps = lax.optimization_barrier((first_other, second, keeps))
-    others = (first_other, swap(second))
+    first_other, keeps = lax.optimization_barrier((first_other, keeps))
+    other = first_other
 
     n = 4 * n_tok
     widths = tuple(count * BLK for _, count in chunks)
     w = 3 * sum(widths)
     weights, windows = [], []
-    for keep, other, width in zip(keeps, others, widths):
+    for keep, width in zip(keeps, widths):
         ins = (acts, keep, other, *windows[1:2])
         *parts, own = call(
             functools.partial(partial_kernel, width),
@@ -237,8 +237,11 @@
             specs=[VMEM] + [ANY] * (len(ins) - 1),
             scratch=[pltpu.VMEM(keep.shape, BF16)] * 2 + [pltpu.SemaphoreType.DMA((2,))],
         )
+        weights += [keep, other]
+        if len(weights) < 2 * len(widths):
+            own, second = lax.optimization_barrier((own, second))
+            other = swap(second)
         windows += [own, *exchange(parts)]
-        weights += [keep, other]
     here, ahead, far, behind = call(
         window_kernel,
         [((n_tok, w), F32)] * 2 + [((n_tok, w), BF16)] * 2,

time: 161 us -> 166 us (1.031)
  starting transfers between devices: 78.8 us -> 90.3 us
  waiting for transfers between devices: 43.4 us -> 39.3 us
  blocking collectives: 25.4 us -> 23.4 us
    ppermute x15, starting transfers between devices: 62.4 us -> 76.1 us  [along_z(): return lax.ppermute(x, Z + ('core',), pairs)]
    ppermute x15, waiting for transfers between devices: 29.8 us -> 22.6 us  [along_z(): return lax.ppermute(x, Z + ('core',), pairs)]
    all_to_all x1, waiting for transfers between devices: 12.9 us -> 16 us  [shards(): lax.all_to_all(jnp.broadcast_to(acts[None], (32,) + acts.shape), ('xl',)...]
    ppermute x2, starting transfers between devices: 7.94 us -> 5.87 us  [swap(): return lax.ppermute(x, 'xl', [(0, 1), (1, 0)])]
    all_to_all x1, blocking collectives: 25.4 us -> 23.4 us  [shards(): lax.all_to_all(shares.reshape(32, n_tok, 2 * depth), ('xl',) + TP, 0, 0,...]
  transfers between devices with their start and end apart: 18 -> 18, of which waited for: 10 -> 10; matrix products, arithmetic and copies ran while one was open for 1% -> 1% of each run, Pallas kernels for 3% -> 2%
where the time goes in v4:
time: 166 us
  starting transfers between devices  90.3 us (54%)
  waiting for transfers between devices  39.3 us (24%)
  blocking collectives  23.4 us (14%)
  Pallas kernels  9.59 us (6%)
  local copies, waits for them, and re-layouts  2.01 us (1%)
    ppermute x15, starting transfers between devices, along_z(): return lax.ppermute(x, Z + ('core',), pairs)  76.1 us
    all_to_all x1, blocking collectives, shards(): lax.all_to_all(shares.reshape(32, n_tok, 2 * depth), ('xl',) + TP, 0, 0,...  23.4 us
    ppermute x15, waiting for transfers between devices, along_z(): return lax.ppermute(x, Z + ('core',), pairs)  22.6 us
    all_to_all x1, waiting for transfers between devices, shards(): lax.all_to_all(jnp.broadcast_to(acts[None], (32,) + acts.shape), ('xl',)...  16 us
    pallas_call x8, Pallas kernels, call(): pl.pallas_call(body, out_shape=[jax.ShapeDtypeStruct(s, d) for s, d in ou...  9.59 us
    all_to_all x1, starting transfers between devices, shards(): lax.all_to_all(jnp.broadcast_to(acts[None], (32,) + acts.shape), ('xl',)...  8.39 us
    ppermute x2, starting transfers between devices, swap(): return lax.ppermute(x, 'xl', [(0, 1), (1, 0)])  5.87 us
  transfers between devices with their start and end apart: 18, of which 10 were waited for; matrix products, arithmetic and copies ran while one was open for 1% of the time, Pallas kernels for 2%

profile of v4, /device:TPU:1, one launch (start us, length us, event | category | flops | bytes accessed | tf_op | source)
XLA Modules:
  0.0 165.6 jit_solution(15953086892816278467)
XLA Ops:
  0.6 2.6 %scaled.2 = (bf16[768,512]{1,0:T(8,128)(2,1)}, bf16[768,384]{1,0:T(8,128)(2,1)}) custom-call(f32[2,14]{1,0:T(2,128)} %refs_0_.3, f32[2,14]{1,0:T(2,128)} %refs_1_.3, f32[2,14]{1,0:T(2,128)} %bitcast.10, bf16[256,1792]{1,0:T(8,128)(2,1)} %refs_3_.3, bf16[256,1792]{1,0:T(8,128)(2,1)} %refs_4_.3, bf16[1792,256]{1,0:T(8,128)(2,1)} %refs_5_.3), custom_call_target="tpu_custom_call" | custom-call | tf_op jit(solution)/shard_map/scaled/pallas_call | solution.py:21
  3.2 3.9 %collective-permute-start = (bf16[768,512]{1,0:T(8,128)(2,1)}, bf16[768,512]{1,0:T(8,128)(2,1)S(1)}, u32[]{:S(2)}, u32[]{:S(2)}) collective-permute-start(bf16[768,512]{1,0:T(8,128)(2,1)} %get-tuple-element.29), channel_id=1, source_target_pairs={{0,16},{16,0},{1,17},{17,1},{2,18},{18,2},{3,19},{19,3},{4,20},{20... | collective-permute-start | bytes 2359304 | tf_op jit(solution)/shard_map/ppermute | solution.py:213
  8.1 8.4 %all-to-all-start = ((bf16[32,2,16,256]{3,2,1,0:T(8,128)(2,1)}), bf16[32,2,16,256]{3,2,1,0:T(8,128)(2,1)S(1)}, u32[]{:S(2)}, u32[]{:S(2)}) async-start(bf16[32,2,16,256]{3,2,1,0:T(8,128)(2,1)} %broadcast_in_dim.2), calls=%async_computation | async-start | bytes 1048576 | tf_op jit(solution)/shard_map/all_to_all | solution.py:220
  16.5 2.6 %scaled.3 = (bf16[768,512]{1,0:T(8,128)(2,1)}, bf16[768,384]{1,0:T(8,128)(2,1)}) custom-call(f32[2,14]{1,0:T(2,128)} %refs_0_.3, f32[2,14]{1,0:T(2,128)} %refs_1_.3, f32[2,14]{1,0:T(2,128)} %bitcast.11, bf16[256,1792]{1,0:T(8,128)(2,1)} %refs_3_.3, bf16[256,1792]{1,0:T(8,128)(2,1)} %refs_4_.3, bf16[1792,256]{1,0:T(8,128)(2,1)} %refs_5_.3), custom_call_target="tpu_custom_call" | custom-call | tf_op jit(solution)/shard_map/scaled/pallas_call | solution.py:21
  19.7 16.0 %all-to-all-done = bf16[32,2,16,256]{3,2,1,0:T(8,128)(2,1)S(1)} async-done(((bf16[32,2,16,256]{3,2,1,0:T(8,128)(2,1)}), bf16[32,2,16,256]{3,2,1,0:T(8,128)(2,1)S(1)}, u32[]{:S(2)}, u32[]{:S(2)}) %all-to-all-start) | async-done | bytes 524320 | tf_op jit(solution)/shard_map/all_to_all | solution.py:220
  38.2 1.9 %collective-permute-start.4 = (bf16[768,384]{1,0:T(8,128)(2,1)S(1)}, bf16[768,384]{1,0:T(8,128)(2,1)S(1)}, u32[]{:S(2)}, u32[]{:S(2)}) collective-permute-start(bf16[768,384]{1,0:T(8,128)(2,1)S(1)} %copy-done.5), channel_id=1, source_target_pairs={{0,16},{16,0},{1,17},{17,1},{2,18},{18,2},{3,19},{19,3},{4,20},{20... | collective-permute-start | bytes 1769480 | tf_op jit(solution)/shard_map/ppermute | solution.py:213
  40.1 11.1 %collective-permute-start.1 = (bf16[64,1536]{1,0:T(8,128)(2,1)S(1)}, bf16[64,1536]{1,0:T(8,128)(2,1)S(1)}, u32[]{:S(2)}, u32[]{:S(2)}) collective-permute-start(bf16[64,1536]{1,0:T(8,128)(2,1)S(1)} %get-tuple-element.37), channel_id=1, source_target_pairs={{0,32},{1,481},{32,64},{33,1},{64,96},{65,33},{96,128},{97,65},{12... | collective-permute-start | bytes 589832 | tf_op jit(solution)/shard_map/ppermute | solution.py:184
  51.2 1.9 %collective-permute-start.2 = (bf16[64,1536]{1,0:T(8,128)(2,1)S(1)}, bf16[64,1536]{1,0:T(8,128)(2,1)S(1)}, u32[]{:S(2)}, u32[]{:S(2)}) collective-permute-start(bf16[64,1536]{1,0:T(8,128)(2,1)S(1)} %get-tuple-element.38), channel_id=1, source_target_pairs={{0,480},{1,33},{32,0},{33,65},{64,32},{65,97},{96,64},{97,129},{12... | collective-permute-start | bytes 589832 | tf_op jit(solution)/shard_map/ppermute | solution.py:184
  53.2 3.8 %collective-permute-start.3 = (bf16[64,1536]{1,0:T(8,128)(2,1)S(1)}, bf16[64,1536]{1,0:T(8,128)(2,1)S(1)}, u32[]{:S(2)}, u32[]{:S(2)}) collective-permute-start(bf16[64,1536]{1,0:T(8,128)(2,1)S(1)} %get-tuple-element.39), channel_id=1, source_target_pairs={{0,64},{1,449},{32,96},{33,481},{64,128},{65,1},{96,160},{97,33},{... | collective-permute-start | bytes 589832 | tf_op jit(solution)/shard_map/ppermute | solution.py:184
  58.1 9.0 %collective-permute-start.5 = (bf16[64,1152]{1,0:T(8,128)(2,1)S(1)}, bf16[64,1152]{1,0:T(8,128)(2,1)S(1)}, u32[]{:S(2)}, u32[]{:S(2)}) collective-permute-start(bf16[64,1152]{1,0:T(8,128)(2,1)S(1)} %get-tuple-element.43), channel_id=1, source_target_pairs={{0,32},{1,481},{32,64},{33,1},{64,96},{65,33},{96,128},{97,65},{12... | collective-permute-start | bytes 442376 | tf_op jit(solution)/shard_map/ppermute | solution.py:184
  69.0 3.8 %collective-permute-start.7 = (bf16[64,1152]{1,0:T(8,128)(2,1)S(1)}, bf16[64,1152]{1,0:T(8,128)(2,1)S(1)}, u32[]{:S(2)}, u32[]{:S(2)}) collective-permute-start(bf16[64,1152]{1,0:T(8,128)(2,1)S(1)} %get-tuple-element.45), channel_id=1, source_target_pairs={{0,64},{1,449},{32,96},{33,481},{64,128},{65,1},{96,160},{97,33},{... | collective-permute-start | bytes 442376 | tf_op jit(solution)/shard_map/ppermute | solution.py:184
  76.1 6.9 %collective-permute-start.9 = (bf16[16,2688]{1,0:T(8,128)(2,1)S(1)}, bf16[16,2688]{1,0:T(8,128)(2,1)S(1)}, u32[]{:S(2)}, u32[]{:S(2)}) collective-permute-start(bf16[16,2688]{1,0:T(8,128)(2,1)S(1)} %get-tuple-element.49), channel_id=1, source_target_pairs={{0,128},{1,385},{32,160},{33,417},{64,192},{65,449},{96,224},{97,4... | collective-permute-start | bytes 258056 | tf_op jit(solution)/shard_map/ppermute | solution.py:184
  83.0 2.4 %collective-permute-start.8 = (bf16[16,2688]{1,0:T(8,128)(2,1)S(1)}, bf16[16,2688]{1,0:T(8,128)(2,1)S(1)}, u32[]{:S(2)}, u32[]{:S(2)}) collective-permute-start(bf16[16,2688]{1,0:T(8,128)(2,1)S(1)} %get-tuple-element.47), channel_id=1, source_target_pairs={{0,384},{1,129},{32,416},{33,161},{64,448},{65,193},{96,480},{97,2... | collective-permute-start | bytes 258056 | tf_op jit(solution)/shard_map/ppermute | solution.py:184
  87.0 6.9 %collective-permute-start.10 = (bf16[16,2688]{1,0:T(8,128)(2,1)S(1)}, bf16[16,2688]{1,0:T(8,128)(2,1)S(1)}, u32[]{:S(2)}, u32[]{:S(2)}) collective-permute-start(bf16[16,2688]{1,0:T(8,128)(2,1)S(1)} %add_convert_fusion), channel_id=1, source_target_pairs={{0,128},{1,385},{32,160},{33,417},{64,192},{65,449},{96,224},{97,4... | collective-permute-start | bytes 258056 | tf_op jit(solution)/shard_map/ppermute | solution.py:184
  93.9 2.8 %collective-permute-done.8.direct = bf16[16,2688]{1,0:T(8,128)(2,1)S(1)} collective-permute-done((bf16[16,2688]{1,0:T(8,128)(2,1)S(1)}, bf16[16,2688]{1,0:T(8,128)(2,1)S(1)}, u32[]{:S(2)}, u32[]{:S(2)}) %collective-permute-start.8) | collective-permute-done | bytes 86048 | tf_op jit(solution)/shard_map/ppermute | solution.py:184
  96.7 2.9 %collective-permute-done.10.passed = bf16[16,2688]{1,0:T(8,128)(2,1)S(1)} collective-permute-done((bf16[16,2688]{1,0:T(8,128)(2,1)S(1)}, bf16[16,2688]{1,0:T(8,128)(2,1)S(1)}, u32[]{:S(2)}, u32[]{:S(2)}) %collective-permute-start.10) | collective-permute-done | bytes 86048 | tf_op jit(solution)/shard_map/ppermute | solution.py:184
  99.6 5.8 %collective-permute-start.11 = (bf16[16,2688]{1,0:T(8,128)(2,1)S(1)}, bf16[16,2688]{1,0:T(8,128)(2,1)S(1)}, u32[]{:S(2)}, u32[]{:S(2)}) collective-permute-start(bf16[16,2688]{1,0:T(8,128)(2,1)S(1)} %gated.1), channel_id=1, source_target_pairs={{0,128},{1,385},{32,160},{33,417},{64,192},{65,449},{96,224},{97,4... | collective-permute-start | bytes 258056 | tf_op jit(solution)/shard_map/ppermute | solution.py:184
  105.5 3.4 %collective-permute-start.13 = (bf16[16,2688]{1,0:T(8,128)(2,1)S(1)}, bf16[16,2688]{1,0:T(8,128)(2,1)S(1)}, u32[]{:S(2)}, u32[]{:S(2)}) collective-permute-start(bf16[16,2688]{1,0:T(8,128)(2,1)S(1)} %gated.1), channel_id=1, source_target_pairs={{0,384},{1,129},{32,416},{33,161},{64,448},{65,193},{96,480},{97,2... | collective-permute-start | bytes 258056 | tf_op jit(solution)/shard_map/ppermute | solution.py:184
  108.9 6.5 %collective-permute-start.12 = (bf16[16,2688]{1,0:T(8,128)(2,1)S(1)}, bf16[16,2688]{1,0:T(8,128)(2,1)S(1)}, u32[]{:S(2)}, u32[]{:S(2)}) collective-permute-start(bf16[16,2688]{1,0:T(8,128)(2,1)S(1)} %collective-permute-done.11), channel_id=1, source_target_pairs={{0,128},{1,385},{32,160},{33,417},{64,192},{65,449},{96,224},{97,4... | collective-permute-start | bytes 258056 | tf_op jit(solution)/shard_map/ppermute | solution.py:184
  115.3 3.4 %collective-permute-done.13 = bf16[16,2688]{1,0:T(8,128)(2,1)S(1)} collective-permute-done((bf16[16,2688]{1,0:T(8,128)(2,1)S(1)}, bf16[16,2688]{1,0:T(8,128)(2,1)S(1)}, u32[]{:S(2)}, u32[]{:S(2)}) %collective-permute-start.13) | collective-permute-done | bytes 86048 | tf_op jit(solution)/shard_map/ppermute | solution.py:184
  119.3 2.2 %collective-permute-start.16 = (bf16[64,2688]{1,0:T(8,128)(2,1)S(1)}, bf16[64,2688]{1,0:T(8,128)(2,1)S(1)}, u32[]{:S(2)}, u32[]{:S(2)}) collective-permute-start(bf16[64,2688]{1,0:T(8,128)(2,1)S(1)} %pad_maximum_fusion.own), channel_id=1, source_target_pairs={{0,64},{1,449},{32,96},{33,481},{64,128},{65,1},{96,160},{97,33},{... | collective-permute-start | bytes 1032200 | tf_op jit(solution)/shard_map/ppermute | solution.py:184
  121.5 8.5 %collective-permute-start.15 = (bf16[64,2688]{1,0:T(8,128)(2,1)S(1)}, bf16[64,2688]{1,0:T(8,128)(2,1)S(1)}, u32[]{:S(2)}, u32[]{:S(2)}) collective-permute-start(bf16[64,2688]{1,0:T(8,128)(2,1)S(1)} %pad_maximum_fusion.own), channel_id=1, source_target_pairs={{0,480},{1,33},{32,0},{33,65},{64,32},{65,97},{96,64},{97,129},{12... | collective-permute-start | bytes 1032200 | tf_op jit(solution)/shard_map/ppermute | solution.py:184
  132.0 8.5 %collective-permute-done.15.behind = bf16[64,2688]{1,0:T(8,128)(2,1)S(1)} collective-permute-done((bf16[64,2688]{1,0:T(8,128)(2,1)S(1)}, bf16[64,2688]{1,0:T(8,128)(2,1)S(1)}, u32[]{:S(2)}, u32[]{:S(2)}) %collective-permute-start.15) | collective-permute-done | bytes 344096 | tf_op jit(solution)/shard_map/ppermute | solution.py:184
  141.6 23.4 %all_to_all.10.parts = bf16[32,16,512]{2,1,0:T(8,128)(2,1)S(1)} all-to-all(bf16[32,16,512]{2,1,0:T(8,128)(2,1)S(1)} %bitcast.7), channel_id=1, replica_groups=mesh['zh'=4,'zl'=4,'xl'=2,'xh'=2,'y'=4,'core'=2] {'xl','xh','y','core'}, dimensions={0} | all-to-all | bytes 1048576 | tf_op jit(solution)/shard_map/all_to_all | solution.py:267
  (37 shorter events, 16.1 us)
Async XLA Ops:
  0.6 6.6 %copy-start.3 = (bf16[16,256]{1,0:T(8,128)(2,1)S(1)}, bf16[16,256]{1,0:T(8,128)(2,1)}, u32[]{:S(2)}) copy-start(bf16[16,256]{1,0:T(8,128)(2,1)} %param.9) | copy-start | bytes 24580
  0.6 6.6 %copy-start.4 = (bf16[16,256]{1,0:T(8,128)(2,1)S(1)}, bf16[16,256]{1,0:T(8,128)(2,1)}, u32[]{:S(2)}) copy-start(bf16[16,256]{1,0:T(8,128)(2,1)} %param.8) | copy-start | bytes 24580
  3.2 16.5 %collective-permute-start = (bf16[768,512]{1,0:T(8,128)(2,1)}, bf16[768,512]{1,0:T(8,128)(2,1)S(1)}, u32[]{:S(2)}, u32[]{:S(2)}) collective-permute-start(bf16[768,512]{1,0:T(8,128)(2,1)} %get-tuple-element.29), channel_id=1, source_target_pairs={{0,16},{16,0},{1,17},{17,1},{2,18},{18,2},{3,19},{19,3},{4,20},{20... | collective-permute-start | bytes 2359304 | tf_op jit(solution)/shard_map/ppermute | solution.py:213
  8.1 27.6 %all-to-all-start = ((bf16[32,2,16,256]{3,2,1,0:T(8,128)(2,1)}), bf16[32,2,16,256]{3,2,1,0:T(8,128)(2,1)S(1)}, u32[]{:S(2)}, u32[]{:S(2)}) async-start(bf16[32,2,16,256]{3,2,1,0:T(8,128)(2,1)} %broadcast_in_dim.2), calls=%async_computation | async-start | bytes 1048576 | tf_op jit(solution)/shard_map/all_to_all | solution.py:220
  35.7 1.1 copy-start
  36.8 1.3 copy-start.5
  36.8 20.2 %copy-start.2 = (bf16[768,384]{1,0:T(8,128)(2,1)S(1)}, bf16[768,384]{1,0:T(8,128)(2,1)}, u32[]{:S(2)}) copy-start(bf16[768,384]{1,0:T(8,128)(2,1)} %get-tuple-element.40.keep_in.refs_2_) | copy-start | bytes 1769476
  38.2 18.8 %collective-permute-start.4 = (bf16[768,384]{1,0:T(8,128)(2,1)S(1)}, bf16[768,384]{1,0:T(8,128)(2,1)S(1)}, u32[]{:S(2)}, u32[]{:S(2)}) collective-permute-start(bf16[768,384]{1,0:T(8,128)(2,1)S(1)} %copy-done.5), channel_id=1, source_target_pairs={{0,16},{16,0},{1,17},{17,1},{2,18},{18,2},{3,19},{19,3},{4,20},{20... | collective-permute-start | bytes 1769480 | tf_op jit(solution)/shard_map/ppermute | solution.py:213
  40.1 16.9 %collective-permute-start.1 = (bf16[64,1536]{1,0:T(8,128)(2,1)S(1)}, bf16[64,1536]{1,0:T(8,128)(2,1)S(1)}, u32[]{:S(2)}, u32[]{:S(2)}) collective-permute-start(bf16[64,1536]{1,0:T(8,128)(2,1)S(1)} %get-tuple-element.37), channel_id=1, source_target_pairs={{0,32},{1,481},{32,64},{33,1},{64,96},{65,33},{96,128},{97,65},{12... | collective-permute-start | bytes 589832 | tf_op jit(solution)/shard_map/ppermute | solution.py:184
  51.2 21.6 %collective-permute-start.2 = (bf16[64,1536]{1,0:T(8,128)(2,1)S(1)}, bf16[64,1536]{1,0:T(8,128)(2,1)S(1)}, u32[]{:S(2)}, u32[]{:S(2)}) collective-permute-start(bf16[64,1536]{1,0:T(8,128)(2,1)S(1)} %get-tuple-element.38), channel_id=1, source_target_pairs={{0,480},{1,33},{32,0},{33,65},{64,32},{65,97},{96,64},{97,129},{12... | collective-permute-start | bytes 589832 | tf_op jit(solution)/shard_map/ppermute | solution.py:184
  53.2 19.7 %collective-permute-start.3 = (bf16[64,1536]{1,0:T(8,128)(2,1)S(1)}, bf16[64,1536]{1,0:T(8,128)(2,1)S(1)}, u32[]{:S(2)}, u32[]{:S(2)}) collective-permute-start(bf16[64,1536]{1,0:T(8,128)(2,1)S(1)} %get-tuple-element.39), channel_id=1, source_target_pairs={{0,64},{1,449},{32,96},{33,481},{64,128},{65,1},{96,160},{97,33},{... | collective-permute-start | bytes 589832 | tf_op jit(solution)/shard_map/ppermute | solution.py:184
  58.1 14.7 %collective-permute-start.5 = (bf16[64,1152]{1,0:T(8,128)(2,1)S(1)}, bf16[64,1152]{1,0:T(8,128)(2,1)S(1)}, u32[]{:S(2)}, u32[]{:S(2)}) collective-permute-start(bf16[64,1152]{1,0:T(8,128)(2,1)S(1)} %get-tuple-element.43), channel_id=1, source_target_pairs={{0,32},{1,481},{32,64},{33,1},{64,96},{65,33},{96,128},{97,65},{12... | collective-permute-start | bytes 442376 | tf_op jit(solution)/shard_map/ppermute | solution.py:184
  67.1 7.1 %collective-permute-start.6 = (bf16[64,1152]{1,0:T(8,128)(2,1)S(1)}, bf16[64,1152]{1,0:T(8,128)(2,1)S(1)}, u32[]{:S(2)}, u32[]{:S(2)}) collective-permute-start(bf16[64,1152]{1,0:T(8,128)(2,1)S(1)} %get-tuple-element.44), channel_id=1, source_target_pairs={{0,480},{1,33},{32,0},{33,65},{64,32},{65,97},{96,64},{97,129},{12... | collective-permute-start | bytes 442376 | tf_op jit(solution)/shard_map/ppermute | solution.py:184
  69.0 6.8 %collective-permute-start.7 = (bf16[64,1152]{1,0:T(8,128)(2,1)S(1)}, bf16[64,1152]{1,0:T(8,128)(2,1)S(1)}, u32[]{:S(2)}, u32[]{:S(2)}) collective-permute-start(bf16[64,1152]{1,0:T(8,128)(2,1)S(1)} %get-tuple-element.45), channel_id=1, source_target_pairs={{0,64},{1,449},{32,96},{33,481},{64,128},{65,1},{96,160},{97,33},{... | collective-permute-start | bytes 442376 | tf_op jit(solution)/shard_map/ppermute | solution.py:184
  76.1 64.4 %copy-start.1 = (bf16[768,512]{1,0:T(8,128)(2,1)S(1)}, bf16[768,512]{1,0:T(8,128)(2,1)}, u32[]{:S(2)}) copy-start(bf16[768,512]{1,0:T(8,128)(2,1)} %get-tuple-element.32.keep_in.refs_0_) | copy-start | bytes 2359300
  76.1 10.9 %collective-permute-start.9 = (bf16[16,2688]{1,0:T(8,128)(2,1)S(1)}, bf16[16,2688]{1,0:T(8,128)(2,1)S(1)}, u32[]{:S(2)}, u32[]{:S(2)}) collective-permute-start(bf16[16,2688]{1,0:T(8,128)(2,1)S(1)} %get-tuple-element.49), channel_id=1, source_target_pairs={{0,128},{1,385},{32,160},{33,417},{64,192},{65,449},{96,224},{97,4... | collective-permute-start | bytes 258056 | tf_op jit(solution)/shard_map/ppermute | solution.py:184
  83.0 13.7 %collective-permute-start.8 = (bf16[16,2688]{1,0:T(8,128)(2,1)S(1)}, bf16[16,2688]{1,0:T(8,128)(2,1)S(1)}, u32[]{:S(2)}, u32[]{:S(2)}) collective-permute-start(bf16[16,2688]{1,0:T(8,128)(2,1)S(1)} %get-tuple-element.47), channel_id=1, source_target_pairs={{0,384},{1,129},{32,416},{33,161},{64,448},{65,193},{96,480},{97,2... | collective-permute-start | bytes 258056 | tf_op jit(solution)/shard_map/ppermute | solution.py:184
  87.0 12.6 %collective-permute-start.10 = (bf16[16,2688]{1,0:T(8,128)(2,1)S(1)}, bf16[16,2688]{1,0:T(8,128)(2,1)S(1)}, u32[]{:S(2)}, u32[]{:S(2)}) collective-permute-start(bf16[16,2688]{1,0:T(8,128)(2,1)S(1)} %add_convert_fusion), channel_id=1, source_target_pairs={{0,128},{1,385},{32,160},{33,417},{64,192},{65,449},{96,224},{97,4... | collective-permute-start | bytes 258056 | tf_op jit(solution)/shard_map/ppermute | solution.py:184
  99.6 9.2 %collective-permute-start.11 = (bf16[16,2688]{1,0:T(8,128)(2,1)S(1)}, bf16[16,2688]{1,0:T(8,128)(2,1)S(1)}, u32[]{:S(2)}, u32[]{:S(2)}) collective-permute-start(bf16[16,2688]{1,0:T(8,128)(2,1)S(1)} %gated.1), channel_id=1, source_target_pairs={{0,128},{1,385},{32,160},{33,417},{64,192},{65,449},{96,224},{97,4... | collective-permute-start | bytes 258056 | tf_op jit(solution)/shard_map/ppermute | solution.py:184
  105.5 13.3 %collective-permute-start.13 = (bf16[16,2688]{1,0:T(8,128)(2,1)S(1)}, bf16[16,2688]{1,0:T(8,128)(2,1)S(1)}, u32[]{:S(2)}, u32[]{:S(2)}) collective-permute-start(bf16[16,2688]{1,0:T(8,128)(2,1)S(1)} %gated.1), channel_id=1, source_target_pairs={{0,384},{1,129},{32,416},{33,161},{64,448},{65,193},{96,480},{97,2... | collective-permute-start | bytes 258056 | tf_op jit(solution)/shard_map/ppermute | solution.py:184
  108.9 10.4 %collective-permute-start.12 = (bf16[16,2688]{1,0:T(8,128)(2,1)S(1)}, bf16[16,2688]{1,0:T(8,128)(2,1)S(1)}, u32[]{:S(2)}, u32[]{:S(2)}) collective-permute-start(bf16[16,2688]{1,0:T(8,128)(2,1)S(1)} %collective-permute-done.11), channel_id=1, source_target_pairs={{0,128},{1,385},{32,160},{33,417},{64,192},{65,449},{96,224},{97,4... | collective-permute-start | bytes 258056 | tf_op jit(solution)/shard_map/ppermute | solution.py:184
  119.3 12.7 %collective-permute-start.16 = (bf16[64,2688]{1,0:T(8,128)(2,1)S(1)}, bf16[64,2688]{1,0:T(8,128)(2,1)S(1)}, u32[]{:S(2)}, u32[]{:S(2)}) collective-permute-start(bf16[64,2688]{1,0:T(8,128)(2,1)S(1)} %pad_maximum_fusion.own), channel_id=1, source_target_pairs={{0,64},{1,449},{32,96},{33,481},{64,128},{65,1},{96,160},{97,33},{... | collective-permute-start | bytes 1032200 | tf_op jit(solution)/shard_map/ppermute | solution.py:184
  121.5 19.0 %collective-permute-start.15 = (bf16[64,2688]{1,0:T(8,128)(2,1)S(1)}, bf16[64,2688]{1,0:T(8,128)(2,1)S(1)}, u32[]{:S(2)}, u32[]{:S(2)}) collective-permute-start(bf16[64,2688]{1,0:T(8,128)(2,1)S(1)} %pad_maximum_fusion.own), channel_id=1, source_target_pairs={{0,480},{1,33},{32,0},{33,65},{64,32},{65,97},{96,64},{97,129},{12... | collective-permute-start | bytes 1032200 | tf_op jit(solution)/shard_map/ppermute | solution.py:184
  130.1 10.4 %collective-permute-start.14 = (bf16[64,2688]{1,0:T(8,128)(2,1)S(1)}, bf16[64,2688]{1,0:T(8,128)(2,1)S(1)}, u32[]{:S(2)}, u32[]{:S(2)}) collective-permute-start(bf16[64,2688]{1,0:T(8,128)(2,1)S(1)} %pad_maximum_fusion.own), channel_id=1, source_target_pairs={{0,32},{1,481},{32,64},{33,1},{64,96},{65,33},{96,128},{97,65},{12... | collective-permute-start | bytes 1032200 | tf_op jit(solution)/shard_map/ppermute | solution.py:184

commit v5 on v3

--- a/solution.py
+++ b/solution.py
@@ -220,7 +220,7 @@
     acts = lax.all_to_all(
         jnp.broadcast_to(acts[None], (32,) + acts.shape), ("xl",) + TP, 0, 0, tiled=True
     ).reshape(2, 16, 2, n_tok, depth)
-    first_other, second, keeps = lax.optimization_barrier((first_other, second, keeps))
+    first_other, keeps = lax.optimization_barrier((first_other, keeps))
     others = (first_other, swap(second))
 
     n = 4 * n_tok

time: 161 us -> 161 us (level)
  transfers between devices with their start and end apart: 18 -> 18, of which waited for: 10 -> 9; matrix products, arithmetic and copies ran while one was open for 1% -> 1% of each run, Pallas kernels for 3% -> 3%
where the time goes in v5:
time: 161 us; the launch traced here: 160 us
  starting transfers between devices  78.3 us (49%)
  waiting for transfers between devices  43.9 us (27%)
  blocking collectives  25.4 us (16%)
  Pallas kernels  9.58 us (6%)
  local copies, waits for them, and re-layouts  2.02 us (1%)
    ppermute x15, starting transfers between devices, along_z(): return lax.ppermute(x, Z + ('core',), pairs)  62.4 us
    ppermute x15, waiting for transfers between devices, along_z(): return lax.ppermute(x, Z + ('core',), pairs)  29.8 us
    all_to_all x1, blocking collectives, shards(): lax.all_to_all(shares.reshape(32, n_tok, 2 * depth), ('xl',) + TP, 0, 0,...  25.4 us
    all_to_all x1, waiting for transfers between devices, shards(): lax.all_to_all(jnp.broadcast_to(acts[None], (32,) + acts.shape), ('xl',)...  14.1 us
    pallas_call x8, Pallas kernels, call(): pl.pallas_call(body, out_shape=[jax.ShapeDtypeStruct(s, d) for s, d in ou...  9.58 us
    all_to_all x1, starting transfers between devices, shards(): lax.all_to_all(jnp.broadcast_to(acts[None], (32,) + acts.shape), ('xl',)...  8.52 us
    ppermute x2, starting transfers between devices, swap(): return lax.ppermute(x, 'xl', [(0, 1), (1, 0)])  7.34 us
  transfers between devices with their start and end apart: 18, of which 9 were waited for; matrix products, arithmetic and copies ran while one was open for 1% of the time, Pallas kernels for 3%

profile of v5, /device:TPU:1, one launch (start us, length us, event | category | flops | bytes accessed | tf_op | source)
XLA Modules:
  0.0 160.2 jit_solution(10384761734751970488)
XLA Ops:
  0.6 2.5 %scaled.2 = (bf16[768,512]{1,0:T(8,128)(2,1)}, bf16[768,384]{1,0:T(8,128)(2,1)}) custom-call(f32[2,14]{1,0:T(2,128)} %refs_0_.3, f32[2,14]{1,0:T(2,128)} %refs_1_.3, f32[2,14]{1,0:T(2,128)} %bitcast.10, bf16[256,1792]{1,0:T(8,128)(2,1)} %refs_3_.3, bf16[256,1792]{1,0:T(8,128)(2,1)} %refs_4_.3, bf16[1792,256]{1,0:T(8,128)(2,1)} %refs_5_.3), custom_call_target="tpu_custom_call" | custom-call | tf_op jit(solution)/shard_map/scaled/pallas_call | solution.py:21
  3.2 3.9 %collective-permute-start = (bf16[768,512]{1,0:T(8,128)(2,1)}, bf16[768,512]{1,0:T(8,128)(2,1)S(1)}, u32[]{:S(2)}, u32[]{:S(2)}) collective-permute-start(bf16[768,512]{1,0:T(8,128)(2,1)} %get-tuple-element.27), channel_id=1, source_target_pairs={{0,16},{16,0},{1,17},{17,1},{2,18},{18,2},{3,19},{19,3},{4,20},{20... | collective-permute-start | bytes 2359304 | tf_op jit(solution)/shard_map/ppermute | solution.py:213
  8.1 8.5 %all-to-all-start = ((bf16[32,2,16,256]{3,2,1,0:T(8,128)(2,1)}), bf16[32,2,16,256]{3,2,1,0:T(8,128)(2,1)S(1)}, u32[]{:S(2)}, u32[]{:S(2)}) async-start(bf16[32,2,16,256]{3,2,1,0:T(8,128)(2,1)} %broadcast_in_dim.2), calls=%async_computation | async-start | bytes 1048576 | tf_op jit(solution)/shard_map/all_to_all | solution.py:220
  16.6 3.4 %collective-permute-start.4 = (bf16[768,384]{1,0:T(8,128)(2,1)S(1)}, bf16[768,384]{1,0:T(8,128)(2,1)S(1)}, u32[]{:S(2)}, u32[]{:S(2)}) collective-permute-start(bf16[768,384]{1,0:T(8,128)(2,1)S(1)} %copy-done.5), channel_id=1, source_target_pairs={{0,16},{16,0},{1,17},{17,1},{2,18},{18,2},{3,19},{19,3},{4,20},{20... | collective-permute-start | bytes 1769480 | tf_op jit(solution)/shard_map/ppermute | solution.py:213
  20.0 2.6 %scaled.3 = (bf16[768,512]{1,0:T(8,128)(2,1)}, bf16[768,384]{1,0:T(8,128)(2,1)}) custom-call(f32[2,14]{1,0:T(2,128)} %refs_0_.3, f32[2,14]{1,0:T(2,128)} %refs_1_.3, f32[2,14]{1,0:T(2,128)} %bitcast.11, bf16[256,1792]{1,0:T(8,128)(2,1)} %refs_3_.3, bf16[256,1792]{1,0:T(8,128)(2,1)} %refs_4_.3, bf16[1792,256]{1,0:T(8,128)(2,1)} %refs_5_.3), custom_call_target="tpu_custom_call" | custom-call | tf_op jit(solution)/shard_map/scaled/pallas_call | solution.py:21
  22.6 14.1 %all-to-all-done = bf16[32,2,16,256]{3,2,1,0:T(8,128)(2,1)S(1)} async-done(((bf16[32,2,16,256]{3,2,1,0:T(8,128)(2,1)}), bf16[32,2,16,256]{3,2,1,0:T(8,128)(2,1)S(1)}, u32[]{:S(2)}, u32[]{:S(2)}) %all-to-all-start) | async-done | bytes 524320 | tf_op jit(solution)/shard_map/all_to_all | solution.py:220
  39.1 11.1 %collective-permute-start.1 = (bf16[64,1536]{1,0:T(8,128)(2,1)S(1)}, bf16[64,1536]{1,0:T(8,128)(2,1)S(1)}, u32[]{:S(2)}, u32[]{:S(2)}) collective-permute-start(bf16[64,1536]{1,0:T(8,128)(2,1)S(1)} %get-tuple-element.33), channel_id=1, source_target_pairs={{0,32},{1,481},{32,64},{33,1},{64,96},{65,33},{96,128},{97,65},{12... | collective-permute-start | bytes 589832 | tf_op jit(solution)/shard_map/ppermute | solution.py:184
  52.2 3.8 %collective-permute-start.3 = (bf16[64,1536]{1,0:T(8,128)(2,1)S(1)}, bf16[64,1536]{1,0:T(8,128)(2,1)S(1)}, u32[]{:S(2)}, u32[]{:S(2)}) collective-permute-start(bf16[64,1536]{1,0:T(8,128)(2,1)S(1)} %get-tuple-element.35), channel_id=1, source_target_pairs={{0,64},{1,449},{32,96},{33,481},{64,128},{65,1},{96,160},{97,33},{... | collective-permute-start | bytes 589832 | tf_op jit(solution)/shard_map/ppermute | solution.py:184
  57.1 2.7 %collective-permute-start.5 = (bf16[64,1152]{1,0:T(8,128)(2,1)S(1)}, bf16[64,1152]{1,0:T(8,128)(2,1)S(1)}, u32[]{:S(2)}, u32[]{:S(2)}) collective-permute-start(bf16[64,1152]{1,0:T(8,128)(2,1)S(1)} %get-tuple-element.39), channel_id=1, source_target_pairs={{0,32},{1,481},{32,64},{33,1},{64,96},{65,33},{96,128},{97,65},{12... | collective-permute-start | bytes 442376 | tf_op jit(solution)/shard_map/ppermute | solution.py:184
  59.8 3.1 %collective-permute-start.6 = (bf16[64,1152]{1,0:T(8,128)(2,1)S(1)}, bf16[64,1152]{1,0:T(8,128)(2,1)S(1)}, u32[]{:S(2)}, u32[]{:S(2)}) collective-permute-start(bf16[64,1152]{1,0:T(8,128)(2,1)S(1)} %get-tuple-element.40), channel_id=1, source_target_pairs={{0,480},{1,33},{32,0},{33,65},{64,32},{65,97},{96,64},{97,129},{12... | collective-permute-start | bytes 442376 | tf_op jit(solution)/shard_map/ppermute | solution.py:184
  62.9 4.3 %collective-permute-start.7 = (bf16[64,1152]{1,0:T(8,128)(2,1)S(1)}, bf16[64,1152]{1,0:T(8,128)(2,1)S(1)}, u32[]{:S(2)}, u32[]{:S(2)}) collective-permute-start(bf16[64,1152]{1,0:T(8,128)(2,1)S(1)} %get-tuple-element.41), channel_id=1, source_target_pairs={{0,64},{1,449},{32,96},{33,481},{64,128},{65,1},{96,160},{97,33},{... | collective-permute-start | bytes 442376 | tf_op jit(solution)/shard_map/ppermute | solution.py:184
  67.3 4.1 %collective-permute-done.7.refs_7_ = bf16[64,1152]{1,0:T(8,128)(2,1)S(1)} collective-permute-done((bf16[64,1152]{1,0:T(8,128)(2,1)S(1)}, bf16[64,1152]{1,0:T(8,128)(2,1)S(1)}, u32[]{:S(2)}, u32[]{:S(2)}) %collective-permute-start.7) | collective-permute-done | bytes 147488 | tf_op jit(solution)/shard_map/ppermute | solution.py:184
  71.6 5.0 %collective-permute-start.9 = (bf16[16,2688]{1,0:T(8,128)(2,1)S(1)}, bf16[16,2688]{1,0:T(8,128)(2,1)S(1)}, u32[]{:S(2)}, u32[]{:S(2)}) collective-permute-start(bf16[16,2688]{1,0:T(8,128)(2,1)S(1)} %get-tuple-element.45), channel_id=1, source_target_pairs={{0,128},{1,385},{32,160},{33,417},{64,192},{65,449},{96,224},{97,4... | collective-permute-start | bytes 258056 | tf_op jit(solution)/shard_map/ppermute | solution.py:184
  76.6 4.3 %collective-permute-start.8 = (bf16[16,2688]{1,0:T(8,128)(2,1)S(1)}, bf16[16,2688]{1,0:T(8,128)(2,1)S(1)}, u32[]{:S(2)}, u32[]{:S(2)}) collective-permute-start(bf16[16,2688]{1,0:T(8,128)(2,1)S(1)} %get-tuple-element.43), channel_id=1, source_target_pairs={{0,384},{1,129},{32,416},{33,161},{64,448},{65,193},{96,480},{97,2... | collective-permute-start | bytes 258056 | tf_op jit(solution)/shard_map/ppermute | solution.py:184
  82.7 3.2 %collective-permute-start.10 = (bf16[16,2688]{1,0:T(8,128)(2,1)S(1)}, bf16[16,2688]{1,0:T(8,128)(2,1)S(1)}, u32[]{:S(2)}, u32[]{:S(2)}) collective-permute-start(bf16[16,2688]{1,0:T(8,128)(2,1)S(1)} %add_convert_fusion), channel_id=1, source_target_pairs={{0,128},{1,385},{32,160},{33,417},{64,192},{65,449},{96,224},{97,4... | collective-permute-start | bytes 258056 | tf_op jit(solution)/shard_map/ppermute | solution.py:184
  85.9 2.4 %collective-permute-done.8.direct = bf16[16,2688]{1,0:T(8,128)(2,1)S(1)} collective-permute-done((bf16[16,2688]{1,0:T(8,128)(2,1)S(1)}, bf16[16,2688]{1,0:T(8,128)(2,1)S(1)}, u32[]{:S(2)}, u32[]{:S(2)}) %collective-permute-start.8) | collective-permute-done | bytes 86048 | tf_op jit(solution)/shard_map/ppermute | solution.py:184
  88.2 5.9 %collective-permute-done.10.passed = bf16[16,2688]{1,0:T(8,128)(2,1)S(1)} collective-permute-done((bf16[16,2688]{1,0:T(8,128)(2,1)S(1)}, bf16[16,2688]{1,0:T(8,128)(2,1)S(1)}, u32[]{:S(2)}, u32[]{:S(2)}) %collective-permute-start.10) | collective-permute-done | bytes 86048 | tf_op jit(solution)/shard_map/ppermute | solution.py:184
  96.1 7.3 %collective-permute-start.13 = (bf16[16,2688]{1,0:T(8,128)(2,1)S(1)}, bf16[16,2688]{1,0:T(8,128)(2,1)S(1)}, u32[]{:S(2)}, u32[]{:S(2)}) collective-permute-start(bf16[16,2688]{1,0:T(8,128)(2,1)S(1)} %gated.1), channel_id=1, source_target_pairs={{0,384},{1,129},{32,416},{33,161},{64,448},{65,193},{96,480},{97,2... | collective-permute-start | bytes 258056 | tf_op jit(solution)/shard_map/ppermute | solution.py:184
  103.4 2.8 %collective-permute-start.12 = (bf16[16,2688]{1,0:T(8,128)(2,1)S(1)}, bf16[16,2688]{1,0:T(8,128)(2,1)S(1)}, u32[]{:S(2)}, u32[]{:S(2)}) collective-permute-start(bf16[16,2688]{1,0:T(8,128)(2,1)S(1)} %collective-permute-done.11), channel_id=1, source_target_pairs={{0,128},{1,385},{32,160},{33,417},{64,192},{65,449},{96,224},{97,4... | collective-permute-start | bytes 258056 | tf_op jit(solution)/shard_map/ppermute | solution.py:184
  106.7 7.3 %collective-permute-done.12 = bf16[16,2688]{1,0:T(8,128)(2,1)S(1)} collective-permute-done((bf16[16,2688]{1,0:T(8,128)(2,1)S(1)}, bf16[16,2688]{1,0:T(8,128)(2,1)S(1)}, u32[]{:S(2)}, u32[]{:S(2)}) %collective-permute-start.12) | collective-permute-done | bytes 86048 | tf_op jit(solution)/shard_map/ppermute | solution.py:184
  114.0 2.0 %collective-permute-start.16 = (bf16[64,2688]{1,0:T(8,128)(2,1)S(1)}, bf16[64,2688]{1,0:T(8,128)(2,1)S(1)}, u32[]{:S(2)}, u32[]{:S(2)}) collective-permute-start(bf16[64,2688]{1,0:T(8,128)(2,1)S(1)} %pad_maximum_fusion.own), channel_id=1, source_target_pairs={{0,64},{1,449},{32,96},{33,481},{64,128},{65,1},{96,160},{97,33},{... | collective-permute-start | bytes 1032200 | tf_op jit(solution)/shard_map/ppermute | solution.py:184
  116.1 7.1 %collective-permute-start.15 = (bf16[64,2688]{1,0:T(8,128)(2,1)S(1)}, bf16[64,2688]{1,0:T(8,128)(2,1)S(1)}, u32[]{:S(2)}, u32[]{:S(2)}) collective-permute-start(bf16[64,2688]{1,0:T(8,128)(2,1)S(1)} %pad_maximum_fusion.own), channel_id=1, source_target_pairs={{0,480},{1,33},{32,0},{33,65},{64,32},{65,97},{96,64},{97,129},{12... | collective-permute-start | bytes 1032200 | tf_op jit(solution)/shard_map/ppermute | solution.py:184
  125.1 7.1 %collective-permute-done.15.behind = bf16[64,2688]{1,0:T(8,128)(2,1)S(1)} collective-permute-done((bf16[64,2688]{1,0:T(8,128)(2,1)S(1)}, bf16[64,2688]{1,0:T(8,128)(2,1)S(1)}, u32[]{:S(2)}, u32[]{:S(2)}) %collective-permute-start.15) | collective-permute-done | bytes 344096 | tf_op jit(solution)/shard_map/ppermute | solution.py:184
  134.2 25.4 %all_to_all.10.parts = bf16[32,16,512]{2,1,0:T(8,128)(2,1)S(1)} all-to-all(bf16[32,16,512]{2,1,0:T(8,128)(2,1)S(1)} %bitcast.7), channel_id=1, replica_groups=mesh['zh'=4,'zl'=4,'xl'=2,'xh'=2,'y'=4,'core'=2] {'xl','xh','y','core'}, dimensions={0} | all-to-all | bytes 1048576 | tf_op jit(solution)/shard_map/all_to_all | solution.py:264
  (37 shorter events, 15.4 us)
Async XLA Ops:
  0.6 6.5 %copy-start.3 = (bf16[16,256]{1,0:T(8,128)(2,1)S(1)}, bf16[16,256]{1,0:T(8,128)(2,1)}, u32[]{:S(2)}) copy-start(bf16[16,256]{1,0:T(8,128)(2,1)} %param.9) | copy-start | bytes 24580
  0.6 6.5 %copy-start.4 = (bf16[16,256]{1,0:T(8,128)(2,1)S(1)}, bf16[16,256]{1,0:T(8,128)(2,1)}, u32[]{:S(2)}) copy-start(bf16[16,256]{1,0:T(8,128)(2,1)} %param.8) | copy-start | bytes 24580
  3.2 19.4 %collective-permute-start = (bf16[768,512]{1,0:T(8,128)(2,1)}, bf16[768,512]{1,0:T(8,128)(2,1)S(1)}, u32[]{:S(2)}, u32[]{:S(2)}) collective-permute-start(bf16[768,512]{1,0:T(8,128)(2,1)} %get-tuple-element.27), channel_id=1, source_target_pairs={{0,16},{16,0},{1,17},{17,1},{2,18},{18,2},{3,19},{19,3},{4,20},{20... | collective-permute-start | bytes 2359304 | tf_op jit(solution)/shard_map/ppermute | solution.py:213
  8.1 8.5 %copy-start.5 = (bf16[768,384]{1,0:T(8,128)(2,1)S(1)}, bf16[768,384]{1,0:T(8,128)(2,1)}, u32[]{:S(2)}) copy-start(bf16[768,384]{1,0:T(8,128)(2,1)} %get-tuple-element.37) | copy-start | bytes 1769476
  8.1 28.6 %all-to-all-start = ((bf16[32,2,16,256]{3,2,1,0:T(8,128)(2,1)}), bf16[32,2,16,256]{3,2,1,0:T(8,128)(2,1)S(1)}, u32[]{:S(2)}, u32[]{:S(2)}) async-start(bf16[32,2,16,256]{3,2,1,0:T(8,128)(2,1)} %broadcast_in_dim.2), calls=%async_computation | async-start | bytes 1048576 | tf_op jit(solution)/shard_map/all_to_all | solution.py:220
  16.6 39.4 %collective-permute-start.4 = (bf16[768,384]{1,0:T(8,128)(2,1)S(1)}, bf16[768,384]{1,0:T(8,128)(2,1)S(1)}, u32[]{:S(2)}, u32[]{:S(2)}) collective-permute-start(bf16[768,384]{1,0:T(8,128)(2,1)S(1)} %copy-done.5), channel_id=1, source_target_pairs={{0,16},{16,0},{1,17},{17,1},{2,18},{18,2},{3,19},{19,3},{4,20},{20... | collective-permute-start | bytes 1769480 | tf_op jit(solution)/shard_map/ppermute | solution.py:213
  36.6 1.1 copy-start
  37.8 18.2 %copy-start.2 = (bf16[768,384]{1,0:T(8,128)(2,1)S(1)}, bf16[768,384]{1,0:T(8,128)(2,1)}, u32[]{:S(2)}) copy-start(bf16[768,384]{1,0:T(8,128)(2,1)} %get-tuple-element.36.keep_in.refs_2_) | copy-start | bytes 1769476
  39.1 16.9 %collective-permute-start.1 = (bf16[64,1536]{1,0:T(8,128)(2,1)S(1)}, bf16[64,1536]{1,0:T(8,128)(2,1)S(1)}, u32[]{:S(2)}, u32[]{:S(2)}) collective-permute-start(bf16[64,1536]{1,0:T(8,128)(2,1)S(1)} %get-tuple-element.33), channel_id=1, source_target_pairs={{0,32},{1,481},{32,64},{33,1},{64,96},{65,33},{96,128},{97,65},{12... | collective-permute-start | bytes 589832 | tf_op jit(solution)/shard_map/ppermute | solution.py:184
  50.2 17.0 %collective-permute-start.2 = (bf16[64,1536]{1,0:T(8,128)(2,1)S(1)}, bf16[64,1536]{1,0:T(8,128)(2,1)S(1)}, u32[]{:S(2)}, u32[]{:S(2)}) collective-permute-start(bf16[64,1536]{1,0:T(8,128)(2,1)S(1)} %get-tuple-element.34), channel_id=1, source_target_pairs={{0,480},{1,33},{32,0},{33,65},{64,32},{65,97},{96,64},{97,129},{12... | collective-permute-start | bytes 589832 | tf_op jit(solution)/shard_map/ppermute | solution.py:184
  52.2 15.1 %collective-permute-start.3 = (bf16[64,1536]{1,0:T(8,128)(2,1)S(1)}, bf16[64,1536]{1,0:T(8,128)(2,1)S(1)}, u32[]{:S(2)}, u32[]{:S(2)}) collective-permute-start(bf16[64,1536]{1,0:T(8,128)(2,1)S(1)} %get-tuple-element.35), channel_id=1, source_target_pairs={{0,64},{1,449},{32,96},{33,481},{64,128},{65,1},{96,160},{97,33},{... | collective-permute-start | bytes 589832 | tf_op jit(solution)/shard_map/ppermute | solution.py:184
  57.1 10.1 %collective-permute-start.5 = (bf16[64,1152]{1,0:T(8,128)(2,1)S(1)}, bf16[64,1152]{1,0:T(8,128)(2,1)S(1)}, u32[]{:S(2)}, u32[]{:S(2)}) collective-permute-start(bf16[64,1152]{1,0:T(8,128)(2,1)S(1)} %get-tuple-element.39), channel_id=1, source_target_pairs={{0,32},{1,481},{32,64},{33,1},{64,96},{65,33},{96,128},{97,65},{12... | collective-permute-start | bytes 442376 | tf_op jit(solution)/shard_map/ppermute | solution.py:184
  59.8 7.4 %collective-permute-start.6 = (bf16[64,1152]{1,0:T(8,128)(2,1)S(1)}, bf16[64,1152]{1,0:T(8,128)(2,1)S(1)}, u32[]{:S(2)}, u32[]{:S(2)}) collective-permute-start(bf16[64,1152]{1,0:T(8,128)(2,1)S(1)} %get-tuple-element.40), channel_id=1, source_target_pairs={{0,480},{1,33},{32,0},{33,65},{64,32},{65,97},{96,64},{97,129},{12... | collective-permute-start | bytes 442376 | tf_op jit(solution)/shard_map/ppermute | solution.py:184
  62.9 8.4 %collective-permute-start.7 = (bf16[64,1152]{1,0:T(8,128)(2,1)S(1)}, bf16[64,1152]{1,0:T(8,128)(2,1)S(1)}, u32[]{:S(2)}, u32[]{:S(2)}) collective-permute-start(bf16[64,1152]{1,0:T(8,128)(2,1)S(1)} %get-tuple-element.41), channel_id=1, source_target_pairs={{0,64},{1,449},{32,96},{33,481},{64,128},{65,1},{96,160},{97,33},{... | collective-permute-start | bytes 442376 | tf_op jit(solution)/shard_map/ppermute | solution.py:184
  71.6 61.5 %copy-start.1 = (bf16[768,512]{1,0:T(8,128)(2,1)S(1)}, bf16[768,512]{1,0:T(8,128)(2,1)}, u32[]{:S(2)}) copy-start(bf16[768,512]{1,0:T(8,128)(2,1)} %get-tuple-element.30.keep_in.refs_0_) | copy-start | bytes 2359300
  71.6 11.1 %collective-permute-start.9 = (bf16[16,2688]{1,0:T(8,128)(2,1)S(1)}, bf16[16,2688]{1,0:T(8,128)(2,1)S(1)}, u32[]{:S(2)}, u32[]{:S(2)}) collective-permute-start(bf16[16,2688]{1,0:T(8,128)(2,1)S(1)} %get-tuple-element.45), channel_id=1, source_target_pairs={{0,128},{1,385},{32,160},{33,417},{64,192},{65,449},{96,224},{97,4... | collective-permute-start | bytes 258056 | tf_op jit(solution)/shard_map/ppermute | solution.py:184
  76.6 11.6 %collective-permute-start.8 = (bf16[16,2688]{1,0:T(8,128)(2,1)S(1)}, bf16[16,2688]{1,0:T(8,128)(2,1)S(1)}, u32[]{:S(2)}, u32[]{:S(2)}) collective-permute-start(bf16[16,2688]{1,0:T(8,128)(2,1)S(1)} %get-tuple-element.43), channel_id=1, source_target_pairs={{0,384},{1,129},{32,416},{33,161},{64,448},{65,193},{96,480},{97,2... | collective-permute-start | bytes 258056 | tf_op jit(solution)/shard_map/ppermute | solution.py:184
  82.7 11.4 %collective-permute-start.10 = (bf16[16,2688]{1,0:T(8,128)(2,1)S(1)}, bf16[16,2688]{1,0:T(8,128)(2,1)S(1)}, u32[]{:S(2)}, u32[]{:S(2)}) collective-permute-start(bf16[16,2688]{1,0:T(8,128)(2,1)S(1)} %add_convert_fusion), channel_id=1, source_target_pairs={{0,128},{1,385},{32,160},{33,417},{64,192},{65,449},{96,224},{97,4... | collective-permute-start | bytes 258056 | tf_op jit(solution)/shard_map/ppermute | solution.py:184
  94.2 9.3 %collective-permute-start.11 = (bf16[16,2688]{1,0:T(8,128)(2,1)S(1)}, bf16[16,2688]{1,0:T(8,128)(2,1)S(1)}, u32[]{:S(2)}, u32[]{:S(2)}) collective-permute-start(bf16[16,2688]{1,0:T(8,128)(2,1)S(1)} %gated.1), channel_id=1, source_target_pairs={{0,128},{1,385},{32,160},{33,417},{64,192},{65,449},{96,224},{97,4... | collective-permute-start | bytes 258056 | tf_op jit(solution)/shard_map/ppermute | solution.py:184
  96.1 10.6 %collective-permute-start.13 = (bf16[16,2688]{1,0:T(8,128)(2,1)S(1)}, bf16[16,2688]{1,0:T(8,128)(2,1)S(1)}, u32[]{:S(2)}, u32[]{:S(2)}) collective-permute-start(bf16[16,2688]{1,0:T(8,128)(2,1)S(1)} %gated.1), channel_id=1, source_target_pairs={{0,384},{1,129},{32,416},{33,161},{64,448},{65,193},{96,480},{97,2... | collective-permute-start | bytes 258056 | tf_op jit(solution)/shard_map/ppermute | solution.py:184
  103.4 10.5 %collective-permute-start.12 = (bf16[16,2688]{1,0:T(8,128)(2,1)S(1)}, bf16[16,2688]{1,0:T(8,128)(2,1)S(1)}, u32[]{:S(2)}, u32[]{:S(2)}) collective-permute-start(bf16[16,2688]{1,0:T(8,128)(2,1)S(1)} %collective-permute-done.11), channel_id=1, source_target_pairs={{0,128},{1,385},{32,160},{33,417},{64,192},{65,449},{96,224},{97,4... | collective-permute-start | bytes 258056 | tf_op jit(solution)/shard_map/ppermute | solution.py:184
  114.0 11.1 %collective-permute-start.16 = (bf16[64,2688]{1,0:T(8,128)(2,1)S(1)}, bf16[64,2688]{1,0:T(8,128)(2,1)S(1)}, u32[]{:S(2)}, u32[]{:S(2)}) collective-permute-start(bf16[64,2688]{1,0:T(8,128)(2,1)S(1)} %pad_maximum_fusion.own), channel_id=1, source_target_pairs={{0,64},{1,449},{32,96},{33,481},{64,128},{65,1},{96,160},{97,33},{... | collective-permute-start | bytes 1032200 | tf_op jit(solution)/shard_map/ppermute | solution.py:184
  116.1 16.1 %collective-permute-start.15 = (bf16[64,2688]{1,0:T(8,128)(2,1)S(1)}, bf16[64,2688]{1,0:T(8,128)(2,1)S(1)}, u32[]{:S(2)}, u32[]{:S(2)}) collective-permute-start(bf16[64,2688]{1,0:T(8,128)(2,1)S(1)} %pad_maximum_fusion.own), channel_id=1, source_target_pairs={{0,480},{1,33},{32,0},{33,65},{64,32},{65,97},{96,64},{97,129},{12... | collective-permute-start | bytes 1032200 | tf_op jit(solution)/shard_map/ppermute | solution.py:184
  123.2 9.9 %collective-permute-start.14 = (bf16[64,2688]{1,0:T(8,128)(2,1)S(1)}, bf16[64,2688]{1,0:T(8,128)(2,1)S(1)}, u32[]{:S(2)}, u32[]{:S(2)}) collective-permute-start(bf16[64,2688]{1,0:T(8,128)(2,1)S(1)} %pad_maximum_fusion.own), channel_id=1, source_target_pairs={{0,32},{1,481},{32,64},{33,1},{64,96},{65,33},{96,128},{97,65},{12... | collective-permute-start | bytes 1032200 | tf_op jit(solution)/shard_map/ppermute | solution.py:184
